TPU v7x, 32 devices: a whole 2x2x4 slice. The times are simulated.
32 devices in a mesh: dp: 8 (over z, x), seq: 4 (over y, core).
Axes of the slice: x: 2, y: 2, z: 4, core: 2. Of those that a mesh axis runs over, the one named last changes fastest.
Arguments:
- tokens: bfloat16 [16, 1024, 512], P('dp', 'seq'), may hold values from -6 to 6
- memory: bfloat16 [16, 1024, 512], P('dp', 'seq'), may hold values from -6 to 6
- segment_ids: int32 [16, 1024], P('dp', 'seq'), may hold values from 0 to 7, never falling along the last dimension, each value on 1 to 768 neighbouring positions
- source_ids: int32 [16, 1024], P('dp', 'seq'), may hold values from 0 to 7, as said below
- source_lengths: int32 [16], P('dp'), may hold values from 512 to 1024, as said below
- cotangent: bfloat16 [16, 1024, 512], P('dp', 'seq'), may hold values from -6 to 6
- self_qkv: bfloat16 [512, 1536], replicated, may hold values from -0.25 to 0.25
- self_out: bfloat16 [512, 512], replicated, may hold values from -0.75 to 0.75
- cross_q: bfloat16 [512, 512], replicated, may hold values from -0.25 to 0.25
- cross_kv: bfloat16 [512, 1024], replicated, may hold values from -0.25 to 0.25
- cross_out: bfloat16 [512, 512], replicated, may hold values from -0.75 to 0.75
- ffn_in: bfloat16 [512, 2048], replicated, may hold values from -0.25 to 0.25
- ffn_out: bfloat16 [2048, 512], replicated, may hold values from -0.125 to 0.125
- norm_gains: float32 [3, 512], replicated, may hold values from 0.5 to 1.5
- bias_rows: float32 [10, 512], replicated, may hold values from -1.5 to 1.5
- hidden_bias: float32 [2048], replicated, may hold values from -1.5 to 1.5
Outputs:
- output: bfloat16 [16, 1024, 512], P('dp', 'seq')
- grad_tokens: bfloat16 [16, 1024, 512], P('dp', 'seq')
- grad_memory: bfloat16 [16, 1024, 512], P('dp', 'seq')
- grad_self_qkv: float32 [512, 1536], replicated
- grad_self_out: float32 [512, 512], replicated
- grad_cross_q: float32 [512, 512], replicated
- grad_cross_kv: float32 [512, 1024], replicated
- grad_cross_out: float32 [512, 512], replicated
- grad_ffn_in: float32 [512, 2048], replicated
- grad_ffn_out: float32 [2048, 512], replicated
- grad_norm_gains: float32 [3, 512], replicated
- grad_bias_rows: float32 [10, 512], replicated
- grad_hidden_bias: float32 [2048], replicated
Inputs may be any that keep to these rules, and one draw needn't show every extreme that they name: `segment_ids`: Non-decreasing along each row; every number 0 to 7 occurs in every row. `source_ids`: in each row, positions below the row's source length hold every number 0 to 7 in non-decreasing order, each on at least two positions; later positions hold 7. `source_lengths`: at least one row has length 1024.
All inputs are finite; a program needn't handle non-finite values.
Results may differ from a plain program's by a relative error of at most 0.02.
Values may be sent and summed in bfloat16 or wider, within the bound.
A program may use at most 192 MiB of HBM per device.

v0:
```python
import jax
import jax.numpy as jnp
from jax import lax
from jax.sharding import PartitionSpec as P

HEADS = 8


SCORE_SCALE = 0.125
EPSILON = 1e-05
MASKED = -1000000000.0
HIGHEST_PRECISION = lax.Precision.HIGHEST
ROOT_HALF = 0.7071067811865476
NORMAL_DENSITY = 0.3989422804014327


def split_heads(values):
    return values.reshape(values.shape[0], values.shape[1], HEADS, values.shape[2] // HEADS)


def merge_heads(values):
    return values.reshape(values.shape[0], values.shape[1], values.shape[2] * values.shape[3])


def project(values, weight):
    return jnp.einsum("rtd,de->rte", values, weight, preferred_element_type=jnp.float32)


def weight_grad(left, right):
    return jnp.einsum("rtd,rte->de", left, right, preferred_element_type=jnp.float32)


def input_grad(grad, weight):
    return jnp.einsum("rte,de->rtd", grad, weight, preferred_element_type=jnp.float32)


def exact_weight_grad(left, right):
    return jnp.einsum("rtd,rte->de", left.astype(jnp.float32), right, precision=HIGHEST_PRECISION)


def exact_input_grad(grad, weight):
    return jnp.einsum("rte,de->rtd", grad, weight.astype(jnp.float32), precision=HIGHEST_PRECISION)


def token_sum(values):
    return jnp.sum(values.astype(jnp.float32), axis=(0, 1))


def gelu_slope(values):
    return 0.5 * (1.0 + lax.erf(values * ROOT_HALF)) + values * NORMAL_DENSITY * jnp.exp(
        -0.5 * values * values
    )


def masked_scores(queries, key_rows, allowed):
    scores = (
        jnp.einsum(
            "rqhd,rkhd->rhqk",
            split_heads(queries),
            split_heads(key_rows),
            preferred_element_type=jnp.float32,
        )
        * SCORE_SCALE
    )
    return jnp.where(allowed, scores, MASKED)


def attend(queries, key_rows, value_rows, allowed):
    scores = masked_scores(queries, key_rows, allowed)
    row_peak = jnp.max(scores, axis=-1, keepdims=True)
    log_total = jnp.log(jnp.sum(jnp.exp(scores - row_peak), axis=-1, keepdims=True)) + row_peak
    weights = jnp.exp(scores - log_total).astype(jnp.bfloat16)
    mixed = jnp.einsum(
        "rhqk,rkhd->rqhd", weights, split_heads(value_rows), preferred_element_type=jnp.float32
    )
    return (merge_heads(mixed), log_total)


def attend_back(queries, key_rows, value_rows, allowed, log_total, grad_mixed):
    weights = jnp.exp(masked_scores(queries, key_rows, allowed) - log_total)
    grad_heads = split_heads(grad_mixed)
    grad_weights = jnp.einsum(
        "rqhd,rkhd->rhqk", grad_heads, split_heads(value_rows), preferred_element_type=jnp.float32
    )
    row_inner = jnp.sum(weights * grad_weights, axis=-1, keepdims=True)
    grad_scores = (weights * (grad_weights - row_inner)).astype(jnp.bfloat16)
    grad_query = (
        jnp.einsum(
            "rhqk,rkhd->rqhd",
            grad_scores,
            split_heads(key_rows),
            preferred_element_type=jnp.float32,
        )
        * SCORE_SCALE
    )
    grad_key = (
        jnp.einsum(
            "rhqk,rqhd->rkhd", grad_scores, split_heads(queries), preferred_element_type=jnp.float32
        )
        * SCORE_SCALE
    )
    grad_value = jnp.einsum(
        "rhqk,rqhd->rkhd",
        weights.astype(jnp.bfloat16),
        grad_heads,
        preferred_element_type=jnp.float32,
    )
    return (merge_heads(grad_query), merge_heads(grad_key), merge_heads(grad_value))


def normalize(residual, gain, shift):
    centred = residual - jnp.mean(residual, axis=-1, keepdims=True)
    inverse_root = lax.rsqrt(jnp.mean(centred * centred, axis=-1, keepdims=True) + EPSILON)
    unit_rows = centred * inverse_root
    return (unit_rows * gain + shift, unit_rows, inverse_root)


def normalize_back(grad, unit_rows, inverse_root, gain):
    scaled = grad * gain
    grad_residual = inverse_root * (
        scaled
        - jnp.mean(scaled, axis=-1, keepdims=True)
        - unit_rows * jnp.mean(scaled * unit_rows, axis=-1, keepdims=True)
    )
    return (grad_residual, jnp.sum(grad * unit_rows, axis=(0, 1)), jnp.sum(grad, axis=(0, 1)))


def shards(
    tokens,
    memory,
    segment_ids,
    source_ids,
    source_lengths,
    cotangent,
    self_qkv,
    self_out,
    cross_q,
    cross_kv,
    cross_out,
    ffn_in,
    ffn_out,
    norm_gains,
    bias_rows,
    hidden_bias,
):
    model_width = tokens.shape[2]
    local_len = tokens.shape[1]
    seq_place = lax.axis_index("seq")
    row_segments, row_sources = (
        lax.all_gather(segment_ids, "seq", axis=1, tiled=True),
        lax.all_gather(source_ids, "seq", axis=1, tiled=True),
    )
    query_pos = seq_place * local_len + jnp.arange(local_len, dtype=jnp.int32)
    key_pos = jnp.arange(row_segments.shape[1], dtype=jnp.int32)
    source_pos = jnp.arange(row_sources.shape[1], dtype=jnp.int32)
    self_allowed = (
        (segment_ids[:, :, None] == row_segments[:, None, :])
        & (query_pos[:, None] >= key_pos[None, :])[None]
    )[:, None]
    cross_allowed = (
        (segment_ids[:, :, None] == row_sources[:, None, :])
        & (source_pos[None, None, :] < source_lengths[:, None, None])
    )[:, None]
    projected = project(tokens, self_qkv)
    queries = (projected[:, :, :model_width] + bias_rows[3]).astype(jnp.bfloat16)
    key_rows = projected[:, :, model_width : 2 * model_width].astype(jnp.bfloat16)
    value_rows = (projected[:, :, 2 * model_width :] + bias_rows[4]).astype(jnp.bfloat16)
    key_full, value_full = (
        lax.all_gather(key_rows, "seq", axis=1, tiled=True),
        lax.all_gather(value_rows, "seq", axis=1, tiled=True),
    )
    attended, self_total = attend(queries, key_full, value_full, self_allowed)
    attended = attended.astype(jnp.bfloat16)
    after_self, unit_first, root_first = normalize(
        tokens.astype(jnp.float32) + project(attended, self_out) + bias_rows[5],
        norm_gains[0],
        bias_rows[0],
    )
    self_low = after_self.astype(jnp.bfloat16)
    cross_query = (project(self_low, cross_q) + bias_rows[6]).astype(jnp.bfloat16)
    row_memory = lax.all_gather(memory, "seq", axis=1, tiled=True)
    key_value = project(row_memory, cross_kv)
    cross_key = key_value[:, :, :model_width].astype(jnp.bfloat16)
    cross_value = (key_value[:, :, model_width:] + bias_rows[7]).astype(jnp.bfloat16)
    crossed, cross_total = attend(cross_query, cross_key, cross_value, cross_allowed)
    crossed = crossed.astype(jnp.bfloat16)
    after_cross, unit_second, root_second = normalize(
        after_self + project(crossed, cross_out) + bias_rows[8], norm_gains[1], bias_rows[1]
    )
    cross_low = after_cross.astype(jnp.bfloat16)
    before = project(cross_low, ffn_in) + hidden_bias
    hidden = jax.nn.gelu(before, approximate=False).astype(jnp.bfloat16)
    output, unit_third, root_third = normalize(
        after_cross + project(hidden, ffn_out) + bias_rows[9], norm_gains[2], bias_rows[2]
    )
    grad_third, gain_third, shift_third = normalize_back(
        cotangent.astype(jnp.float32), unit_third, root_third, norm_gains[2]
    )
    ffn_branch = grad_third.astype(jnp.bfloat16)
    bias_ffn_out = token_sum(ffn_branch)
    grad_ffn_out = weight_grad(hidden, ffn_branch)
    grad_hidden = (input_grad(ffn_branch, ffn_out) * gelu_slope(before)).astype(jnp.bfloat16)
    grad_hbias = token_sum(grad_hidden)
    grad_ffn_in = weight_grad(cross_low, grad_hidden)
    grad_second = grad_third + input_grad(grad_hidden, ffn_in)
    grad_mid, gain_second, shift_second = normalize_back(
        grad_second, unit_second, root_second, norm_gains[1]
    )
    cross_branch = grad_mid.astype(jnp.bfloat16)
    bias_cross_out = token_sum(cross_branch)
    grad_cross_out = weight_grad(crossed, cross_branch)
    grad_crossed = input_grad(cross_branch, cross_out).astype(jnp.bfloat16)
    grad_cquery, grad_ckey, grad_cvalue = attend_back(
        cross_query, cross_key, cross_value, cross_allowed, cross_total, grad_crossed
    )
    grad_cquery = grad_cquery.astype(jnp.bfloat16)
    grad_ckey, grad_cvalue = (
        lax.psum_scatter(
            grad_ckey.astype(jnp.bfloat16), "seq", scatter_dimension=1, tiled=True
        ).astype(jnp.float32),
        lax.psum_scatter(
            grad_cvalue.astype(jnp.bfloat16), "seq", scatter_dimension=1, tiled=True
        ).astype(jnp.float32),
    )
    grad_pair = jnp.concatenate([grad_ckey, grad_cvalue], axis=2)
    bias_cross_value = jnp.sum(grad_cvalue, axis=(0, 1))
    grad_cross_kv = exact_weight_grad(memory, grad_pair)
    grad_memory = exact_input_grad(grad_pair, cross_kv).astype(jnp.bfloat16)
    bias_cross_query = token_sum(grad_cquery)
    grad_cross_q = weight_grad(self_low, grad_cquery)
    grad_first = grad_mid + input_grad(grad_cquery, cross_q)
    grad_start, gain_first, shift_first = normalize_back(
        grad_first, unit_first, root_first, norm_gains[0]
    )
    self_branch = grad_start.astype(jnp.bfloat16)
    bias_self_out = token_sum(self_branch)
    grad_self_out = weight_grad(attended, self_branch)
    grad_attended = input_grad(self_branch, self_out).astype(jnp.bfloat16)
    grad_query, grad_key, grad_value = attend_back(
        queries, key_full, value_full, self_allowed, self_total, grad_attended
    )
    grad_key, grad_value = (
        lax.psum_scatter(
            grad_key.astype(jnp.bfloat16), "seq", scatter_dimension=1, tiled=True
        ).astype(jnp.float32),
        lax.psum_scatter(
            grad_value.astype(jnp.bfloat16), "seq", scatter_dimension=1, tiled=True
        ).astype(jnp.float32),
    )
    joined = jnp.concatenate(
        [
            grad_query.astype(jnp.bfloat16),
            grad_key.astype(jnp.bfloat16),
            grad_value.astype(jnp.bfloat16),
        ],
        axis=2,
    )
    bias_query = token_sum(joined[:, :, :model_width])
    bias_value = token_sum(joined[:, :, 2 * model_width :])
    grad_self_qkv = weight_grad(tokens, joined)
    grad_tokens = (grad_start + input_grad(joined, self_qkv)).astype(jnp.bfloat16)
    reduced = lax.psum(
        (
            grad_self_qkv,
            grad_self_out,
            grad_cross_q,
            grad_cross_kv,
            grad_cross_out,
            grad_ffn_in,
            grad_ffn_out,
            jnp.stack([gain_first, gain_second, gain_third]),
            jnp.stack(
                [
                    shift_first,
                    shift_second,
                    shift_third,
                    bias_query,
                    bias_value,
                    bias_self_out,
                    bias_cross_query,
                    bias_cross_value,
                    bias_cross_out,
                    bias_ffn_out,
                ]
            ),
            grad_hbias,
        ),
        ("dp", "seq"),
    )
    return (
        output.astype(jnp.bfloat16),
        grad_tokens,
        grad_memory,
        reduced[0],
        reduced[1],
        reduced[2],
        reduced[3],
        reduced[4],
        reduced[5],
        reduced[6],
        reduced[7],
        reduced[8],
        reduced[9],
    )


def solution(mesh):
    placed = (
        P("dp", "seq", None),
        P("dp", "seq", None),
        P("dp", "seq"),
        P("dp", "seq"),
        P("dp"),
        P("dp", "seq", None),
        P(),
        P(),
        P(),
        P(),
        P(),
        P(),
        P(),
        P(),
        P(),
        P(),
    )
    return jax.shard_map(
        shards,
        mesh=mesh,
        in_specs=placed,
        out_specs=(
            P("dp", "seq", None),
            P("dp", "seq", None),
            P("dp", "seq", None),
            P(),
            P(),
            P(),
            P(),
            P(),
            P(),
            P(),
            P(),
            P(),
            P(),
        ),
        check_vma=False,
    )
```

profile of v0, /device:TPU:0, one launch (start us, length us, event | category | flops | bytes accessed | tf_op | source)
XLA Modules:
  0.0 620.2 jit_solution(10564013033178879263)
XLA Ops:
  16.5 6.1 all_gather.16
  22.6 5.4 all_gather.19
  29.7 8.2 %all-gather.6.cloned.1.call-done = bf16[2,1024,512]{2,1,0:T(8,128)(2,1)} async-done(((bf16[2,256,512]{2,1,0:T(8,128)(2,1)}), bf16[2,1024,512]{2,1,0:T(8,128)(2,1)}) %all-gather.6.cloned.1.call-update) | async-done | bytes 2097168 | tf_op jit(solution)/shard_map/all_gather | solution.py:169
  38.0 3.9 copy.60
  41.9 4.5 fusion
  46.4 6.0 copy-done.2
  52.4 4.4 exponential_reduce_fusion.1
  56.8 6.0 all-gather.4.cloned.1.call-done
  66.7 9.6 %convolution_convert_fusion.5 = bf16[2,8,64,256]{3,2,1,0:T(8,128)(2,1)S(1)} fusion(bf16[2,1024,8,64]{1,3,2,0:T(8,128)(2,1)} %bitcast.180, f32[2,8,256,1024]{3,2,1,0:T(8,128)} %copy-done.2, f32[2,8,256]{2,1,0:T(8,128)S(1)} %log_add_fusion.1, pred[2,256,1024]{2,1,0:T(8,128)(4,1)S(1)} %get-tuple-element.86), kind=kOutput, calls=%fused_computation.97 | convolution fusion | flops 553910272 | bytes 19939328 | tf_op jit(solution)/shard_map/rhqk,rkhd->rqhd/dot_general | solution.py:73
  80.8 6.1 all-gather.8.cloned.1.call-done
  86.9 4.3 fusion.64
  97.7 4.4 exponential_reduce_fusion
  102.1 4.9 copy-done.24
  108.6 6.0 convolution_convert_fusion.4
  118.2 9.8 %fusion.6 = bf16[2,256,2048]{2,1,0:T(8,128)(2,1)S(1)} fusion(f32[2,256,2048]{2,1,0:T(8,128)S(1)} %get-tuple-element.95, f32[2048]{0:T(1024)S(1)} %copy-done.50, u8[256,2048]{1,0:T(8,128)(4,1)S(1)} %get-tuple-element.40, u8[256,2048]{1,0:T(8,128)(4,1)S(1)} %get-tuple-element.39), kind=kLoop, calls=%fused_computation.18 | loop fusion | flops 74448896 | bytes 7348224 | tf_op jit(solution)/shard_map/convert_element_type | solution.py:192
  137.8 13.7 %multiply_reduce_fusion.1 = (f32[2,8,256]{2,1,0:T(8,128)S(1)}, f32[2,8,256,1024]{3,2,1,0:T(8,128)}) fusion(f32[2,8,256,1024]{3,2,1,0:T(8,128)} %copy-done.3, f32[2,8,256]{2,1,0:T(8,128)S(1)} %log_add_fusion, pred[2,256,1024]{2,1,0:T(8,128)(4,1)S(1)} %copy-done.12, bf16[2,256,8,64]{1,3,2,0:T(8,128)(2,1)S(1)} %bitcast.195, bf16[2,1024,8,64]{1,3,2,0:T(8,128)(2,1)} %bitcast.183), kind=kOutput, calls=%fused_computation.3 | convolution fusion | flops 557838336 | bytes 36732928 | tf_op jit(solution)/shard_map/rqhd,rkhd->rhqk/dot_general | solution.py:82
  151.5 12.1 %multiply_convert_fusion.1 = bf16[2,8,256,1024]{3,2,1,0:T(8,128)(2,1)S(1)} fusion(f32[2,8,256,1024]{3,2,1,0:T(8,128)} %get-tuple-element.100, f32[2,8,256,1024]{3,2,1,0:T(8,128)} %copy-done.3, f32[2,8,256]{2,1,0:T(8,128)S(1)} %get-tuple-element.99, f32[2,8,256]{2,1,0:T(8,128)S(1)} %log_add_fusion, pred[2,256,1024]{2,1,0:T(8,128)(4,1)S(1)} %copy-done.12), kind=kLoop, calls=%fused_computation.2 | loop fusion | flops 25165824 | bytes 42500096 | tf_op jit(solution)/shard_map/convert_element_type | solution.py:86
  169.4 11.9 %convolution_convert_fusion = bf16[2,8,64,1024]{3,2,1,0:T(8,128)(2,1)} fusion(bf16[2,256,8,64]{1,3,2,0:T(8,128)(2,1)} %bitcast.196, f32[2,8,256,1024]{3,2,1,0:T(8,128)} %copy-done.3, f32[2,8,256]{2,1,0:T(8,128)S(1)} %log_add_fusion, pred[2,256,1024]{2,1,0:T(8,128)(4,1)} %get-tuple-element.85), kind=kOutput, calls=%fused_computation.61 | convolution fusion | flops 554696704 | bytes 19939328 | tf_op jit(solution)/shard_map/rhqk,rqhd->rkhd/dot_general | solution.py:102
  181.3 4.1 copy.72
  185.7 6.5 %convert_reduce_fusion.4 = (f32[8,64]{1,0:T(8,128)S(1)}, bf16[2,8,64,256]{3,2,1,0:T(8,128)(2,1)S(1)}) fusion(bf16[2,1024,8,64]{1,3,2,0:T(8,128)(2,1)S(1)} %bitcast.177, bf16[2,8,256,1024]{3,2,1,0:T(8,128)(2,1)} %copy-done.4), kind=kOutput, calls=%fused_computation.115 | convolution fusion | flops 537918976 | bytes 11012096 | tf_op jit(solution)/shard_map/rhqk,rkhd->rqhd/dot_general | solution.py:88
  195.1 9.9 %convolution_convert_fusion.1 = bf16[2,8,64,1024]{3,2,1,0:T(8,128)(2,1)} fusion(bf16[2,256,8,64]{1,3,2,0:T(8,128)(2,1)S(1)} %bitcast.197, f32[2,8,256,1024]{3,2,1,0:T(8,128)} %copy-done.2, f32[2,8,256]{2,1,0:T(8,128)S(1)} %log_add_fusion.1, pred[2,256,1024]{2,1,0:T(8,128)(4,1)S(1)} %copy-done.10), kind=kOutput, calls=%fused_computation.62 | convolution fusion | flops 554696704 | bytes 19939328 | tf_op jit(solution)/shard_map/rhqk,rqhd->rkhd/dot_general | solution.py:102
  205.0 4.0 copy.69
  209.1 14.2 %multiply_reduce_fusion = (f32[2,8,256]{2,1,0:T(8,128)S(1)}, f32[2,8,256,1024]{3,2,1,0:T(8,128)}) fusion(f32[2,8,256,1024]{3,2,1,0:T(8,128)} %copy-done.2, f32[2,8,256]{2,1,0:T(8,128)S(1)} %log_add_fusion.1, pred[2,256,1024]{2,1,0:T(8,128)(4,1)S(1)} %copy-done.10, bf16[2,256,8,64]{1,3,2,0:T(8,128)(2,1)S(1)} %bitcast.198, bf16[2,1024,8,64]{1,3,2,0:T(8,128)(2,1)} %bitcast.181), kind=kOutput, calls=%fused_computation.1 | convolution fusion | flops 557838336 | bytes 36732928 | tf_op jit(solution)/shard_map/rqhd,rkhd->rhqk/dot_general | solution.py:82
  223.3 12.2 %multiply_convert_fusion = bf16[2,8,256,1024]{3,2,1,0:T(8,128)(2,1)S(1)} fusion(f32[2,8,256,1024]{3,2,1,0:T(8,128)} %get-tuple-element.103, f32[2,8,256,1024]{3,2,1,0:T(8,128)} %copy-done.2, f32[2,8,256]{2,1,0:T(8,128)S(1)} %get-tuple-element.102, f32[2,8,256]{2,1,0:T(8,128)S(1)} %log_add_fusion.1, pred[2,256,1024]{2,1,0:T(8,128)(4,1)S(1)} %copy-done.10), kind=kLoop, calls=%fused_computation | loop fusion | flops 25165824 | bytes 42500096 | tf_op jit(solution)/shard_map/convert_element_type | solution.py:86
  239.3 4.1 copy.68
  243.7 7.5 %convert_reduce_fusion.7 = (f32[8,64]{1,0:T(8,128)S(1)}, bf16[2,8,64,256]{3,2,1,0:T(8,128)(2,1)}) fusion(bf16[2,1024,8,64]{1,3,2,0:T(8,128)(2,1)S(1)} %bitcast.175, bf16[2,8,256,1024]{3,2,1,0:T(8,128)(2,1)} %copy-done.5), kind=kOutput, calls=%fused_computation.118 | convolution fusion | flops 537918976 | bytes 11012096 | tf_op jit(solution)/shard_map/rhqk,rkhd->rqhd/dot_general | solution.py:88
  269.9 4.2 fusion.28
  274.1 29.4 %reduce-scatter.5.cloned.1.call-done = bf16[2,256,512]{2,1,0:T(8,128)(2,1)} async-done(((bf16[2,1024,512]{2,1,0:T(8,128)(2,1)}), bf16[2,256,512]{2,1,0:T(8,128)(2,1)}) %reduce-scatter.5.cloned.1.call-update) | async-done | bytes 524304 | tf_op jit(solution)/shard_map/reduce_scatter | solution.py:243
  303.5 4.2 convolution_bitcast_fusion.2
  310.2 42.6 %all-reduce = (f32[3,512]{1,0:T(4,128)}, f32[10,512]{1,0:T(8,128)}, f32[2048]{0:T(1024)}) all-reduce(f32[3,512]{1,0:T(4,128)S(1)} %pad_maximum_fusion.10, f32[10,512]{1,0:T(8,128)S(1)} %stack.59, f32[2048]{0:T(1024)S(1)} %get-tuple-element.108), channel_id=1, replica_groups=mesh['dp'=8,'seq'=4] {'dp','seq'}, use_global_device_ids=true, to_apply=%region_32.33 | all-reduce | flops 8704 | bytes 69632 | tf_op jit(solution)/shard_map/psum | solution.py:262
  356.7 4.4 fusion.50
  361.2 234.8 %all-reduce.4.cloned.1.call-done = (f32[512,1536]{0,1:T(8,128)}, f32[512,512]{1,0:T(8,128)}, f32[512,512]{1,0:T(8,128)}, f32[512,1024]{0,1:T(8,128)}, f32[512,51...) async-done(((f32[512,1536]{0,1:T(8,128)}, f32[512,512]{1,0:T(8,128)}, f32[512,512]{1,0:T(8,128)}, f32[512,1024]{0,1:T(8,128)}, f32[512,512]{1,0:T(8,128)}, ...) | async-done | bytes 16777232 | tf_op jit(solution)/shard_map/psum | solution.py:262
  (203 shorter events, 95.1 us)
Async XLA Ops:
  7.2 108.5 %copy-start = (bf16[512,2048]{1,0:T(8,128)(2,1)S(1)}, bf16[512,2048]{1,0:T(8,128)(2,1)}, u32[]{:S(2)}) copy-start(bf16[512,2048]{1,0:T(8,128)(2,1)} %param.27) | copy-start | bytes 6291460
  7.2 30.8 %all-gather.6.cloned.1.call-start = ((), (), s32[]{:S(2)}) async-start(), calls=%async_computation.5 | async-start | bytes 2621440 | tf_op jit(solution)/shard_map/all_gather | solution.py:169
  11.6 11.0 %copy-start.52 = (s32[2,256]{1,0:T(2,128)S(1)}, s32[2,256]{1,0:T(2,128)}, u32[]{:S(2)}) copy-start(s32[2,256]{1,0:T(2,128)} %param.19) | copy-start | bytes 6148
  11.6 16.4 %copy-start.53 = (s32[2]{0:T(128)S(1)}, s32[2]{0:T(128)}, u32[]{:S(2)}) copy-start(s32[2]{0:T(128)} %param.20) | copy-start | bytes 28
  11.6 16.5 %copy-start.51 = (f32[3,512]{1,0:T(4,128)S(1)}, f32[3,512]{1,0:T(4,128)}, u32[]{:S(2)}) copy-start(f32[3,512]{1,0:T(4,128)} %param.29) | copy-start | bytes 18436
  12.5 50.2 %all-gather.4.cloned.1.call-start = ((), (), s32[]{:S(2)}) async-start(), calls=%async_computation.4 | async-start | bytes 2621440 | tf_op jit(solution)/shard_map/all_gather | solution.py:170
  15.2 71.7 %all-gather.8.cloned.1.call-start = ((), (), s32[]{:S(2)}) async-start(), calls=%async_computation.6 | async-start | bytes 2621440 | tf_op jit(solution)/shard_map/all_gather | solution.py:181
  16.0 251.5 %reduce-scatter.9.cloned.1.call-start = ((), (), s32[]{:S(2)}) async-start(), calls=%async_computation.9 | async-start | bytes 2621440 | tf_op jit(solution)/shard_map/reduce_scatter | solution.py:218
  16.2 30.1 %copy-start.17 = (bf16[2,256,512]{1,2,0:T(8,128)(2,1)}, bf16[2,256,512]{1,2,0:T(8,128)(2,1)S(1)}, u32[]{:S(2)}) copy-start(bf16[2,256,512]{1,2,0:T(8,128)(2,1)S(1)} %copy.59) | copy-start | bytes 1572868
  29.7 36.9 %copy-start.9 = (pred[2,256,1024]{2,1,0:T(8,128)(4,1)}, pred[2,256,1024]{2,1,0:T(8,128)(4,1)S(1)}, u32[]{:S(2)}) copy-start(pred[2,256,1024]{2,1,0:T(8,128)(4,1)S(1)} %get-tuple-element.86) | copy-start | bytes 1572868
  66.7 9.7 %copy-start.27 = (bf16[512,512]{1,0:T(8,128)(2,1)S(1)}, bf16[512,512]{1,0:T(8,128)(2,1)}, u32[]{:S(2)}) copy-start(bf16[512,512]{1,0:T(8,128)(2,1)} %param.23) | copy-start | bytes 1572868
  66.7 9.7 %copy-start.29 = (bf16[2,256,512]{2,1,0:T(8,128)(2,1)S(1)}, bf16[2,256,512]{2,1,0:T(8,128)(2,1)}, u32[]{:S(2)}) copy-start(bf16[2,256,512]{2,1,0:T(8,128)(2,1)} %param.16) | copy-start | bytes 1572868
  66.7 10.7 %copy-start.55 = (bf16[512,512]{1,0:T(8,128)(2,1)S(1)}, bf16[512,512]{1,0:T(8,128)(2,1)}, u32[]{:S(2)}) copy-start(bf16[512,512]{1,0:T(8,128)(2,1)} %param.24) | copy-start | bytes 1572868
  97.7 11.0 %copy-start.3 = (f32[2,8,256,1024]{3,2,1,0:T(8,128)}, f32[2,8,256,1024]{3,2,1,0:T(8,128)S(1)}, u32[]{:S(2)}) copy-start(f32[2,8,256,1024]{3,2,1,0:T(8,128)S(1)} %get-tuple-element.92) | copy-start | bytes 50331652
  97.7 9.3 %copy-start.24 = (f32[2,1024,1024]{1,2,0:T(8,128)S(1)}, f32[2,1024,1024]{1,2,0:T(8,128)}, u32[]{:S(2)}) copy-start(f32[2,1024,1024]{1,2,0:T(8,128)} %copy-done.23) | copy-start | bytes 25165828
  115.3 20.8 %copy-start.14 = (f32[2,256,512]{2,1,0:T(8,128)}, f32[2,256,512]{2,1,0:T(8,128)S(1)}, u32[]{:S(2)}) copy-start(f32[2,256,512]{2,1,0:T(8,128)S(1)} %get-tuple-element.94) | copy-start | bytes 3145732
  118.1 9.9 %copy-start.54 = (bf16[2048,512]{1,0:T(8,128)(2,1)S(1)}, bf16[2048,512]{1,0:T(8,128)(2,1)}, u32[]{:S(2)}) copy-start(bf16[2048,512]{1,0:T(8,128)(2,1)} %param.28) | copy-start | bytes 6291460
  136.5 14.9 %copy-start.21 = (bf16[2,256,512]{2,1,0:T(8,128)(2,1)}, bf16[2,256,512]{2,1,0:T(8,128)(2,1)S(1)}, u32[]{:S(2)}) copy-start(bf16[2,256,512]{2,1,0:T(8,128)(2,1)S(1)} %get-tuple-element.66) | copy-start | bytes 1572868
  137.7 13.7 %copy-start.39 = (bf16[2,256,512]{1,2,0:T(8,128)(2,1)}, bf16[2,256,512]{1,2,0:T(8,128)(2,1)S(1)}, u32[]{:S(2)}) copy-start(bf16[2,256,512]{1,2,0:T(8,128)(2,1)S(1)} %copy.65) | copy-start | bytes 1572868
  151.5 12.1 %copy-start.20 = (bf16[2,256,512]{1,2,0:T(8,128)(2,1)S(1)}, bf16[2,256,512]{1,2,0:T(8,128)(2,1)}, u32[]{:S(2)}) copy-start(bf16[2,256,512]{1,2,0:T(8,128)(2,1)} %copy.63) | copy-start | bytes 1572868
  169.4 99.3 %reduce-scatter.11.cloned.1.call-start = ((), (), s32[]{:S(2)}) async-start(), calls=%async_computation.10 | async-start | bytes 2621440 | tf_op jit(solution)/shard_map/reduce_scatter | solution.py:221
  185.4 88.7 %reduce-scatter.7.cloned.1.call-start = ((), (), s32[]{:S(2)}) async-start(), calls=%async_computation.8 | async-start | bytes 2621440 | tf_op jit(solution)/shard_map/reduce_scatter | solution.py:246
  185.7 6.6 %copy-start.15 = (f32[2,256,512]{2,1,0:T(8,128)S(1)}, f32[2,256,512]{2,1,0:T(8,128)}, u32[]{:S(2)}) copy-start(f32[2,256,512]{2,1,0:T(8,128)} %copy-done.14) | copy-start | bytes 3145732
  185.7 6.6 %copy-start.42 = (f32[2,256,512]{2,1,0:T(8,128)S(1)}, f32[2,256,512]{2,1,0:T(8,128)}, u32[]{:S(2)}) copy-start(f32[2,256,512]{2,1,0:T(8,128)} %copy-done.41) | copy-start | bytes 3145732
  185.7 6.6 %copy-start.56 = (bf16[512,512]{1,0:T(8,128)(2,1)S(1)}, bf16[512,512]{1,0:T(8,128)(2,1)}, u32[]{:S(2)}) copy-start(bf16[512,512]{1,0:T(8,128)(2,1)} %param.24) | copy-start | bytes 1572868
  193.9 11.1 %copy-start.22 = (bf16[2,256,512]{2,1,0:T(8,128)(2,1)}, bf16[2,256,512]{2,1,0:T(8,128)(2,1)S(1)}, u32[]{:S(2)}) copy-start(bf16[2,256,512]{2,1,0:T(8,128)(2,1)S(1)} %get-tuple-element.68) | copy-start | bytes 1572868
  209.0 94.5 %reduce-scatter.5.cloned.1.call-start = ((), (), s32[]{:S(2)}) async-start(), calls=%async_computation.7 | async-start | bytes 2621440 | tf_op jit(solution)/shard_map/reduce_scatter | solution.py:243
  223.3 12.2 %copy-start.18 = (bf16[2,256,512]{1,2,0:T(8,128)(2,1)S(1)}, bf16[2,256,512]{1,2,0:T(8,128)(2,1)}, u32[]{:S(2)}) copy-start(bf16[2,256,512]{1,2,0:T(8,128)(2,1)} %copy-done.17) | copy-start | bytes 1572868
  243.4 352.6 %all-reduce.4.cloned.1.call-start = ((), (), s32[]{:S(2)}) async-start(), calls=%async_computation.11 | async-start | bytes 33554432 | tf_op jit(solution)/shard_map/psum | solution.py:262
  251.2 7.8 %copy-start.31 = (bf16[2,8,64,256]{3,2,1,0:T(8,128)(2,1)S(1)}, bf16[2,8,64,256]{3,2,1,0:T(8,128)(2,1)}, u32[]{:S(2)}) copy-start(bf16[2,8,64,256]{3,2,1,0:T(8,128)(2,1)} %copy-done.30) | copy-start | bytes 1572868
  251.2 9.4 %copy-start.47 = (bf16[2,256,512]{2,1,0:T(8,128)(2,1)S(1)}, bf16[2,256,512]{2,1,0:T(8,128)(2,1)}, u32[]{:S(2)}) copy-start(bf16[2,256,512]{2,1,0:T(8,128)(2,1)} %copy-done.46) | copy-start | bytes 1572868
  253.4 7.3 %copy-start.36 = (bf16[2,256,2048]{2,1,0:T(8,128)(2,1)S(1)}, bf16[2,256,2048]{2,1,0:T(8,128)(2,1)}, u32[]{:S(2)}) copy-start(bf16[2,256,2048]{2,1,0:T(8,128)(2,1)} %copy-done.35) | copy-start | bytes 6291460
  (33 other events, 107.9 us)
Sparse Core Ops, SparseCore 0:
  12.6 25.3 all-gather.5
  40.1 22.5 all-gather.3
  64.3 22.5 all-gather.7
  169.5 31.4 reduce-scatter.8
  203.5 31.3 reduce-scatter.10
  237.3 31.4 reduce-scatter.6
  272.0 31.3 reduce-scatter.4
  311.0 284.9 all-reduce.3
where the time goes:
time: 627 us; the launch traced here: 620 us
  waiting for transfers between devices  285 us (45%)
  matrix products  143 us (23%)
  local copies, waits for them, and re-layouts  64.6 us (10%)
  other arithmetic  57 us (9%)
  blocking collectives  54.2 us (9%)
  between operations  15.5 us (2%)
    psum x1, waiting for transfers between devices, shards(): lax.psum((grad_self_qkv, grad_self_out, grad_cross_q, grad_cross_kv, grad...  235 us
    psum x1, blocking collectives, shards(): lax.psum((grad_self_qkv, grad_self_out, grad_cross_q, grad_cross_kv, grad...  42.6 us
    unnamed x121, local copies, waits for them, and re-layouts  35.8 us
    reduce_scatter x1, waiting for transfers between devices, shards(): lax.psum_scatter(grad_key.astype(jnp.bfloat16), 'seq', scatter_dimension=...  29.4 us
    dot_general x2, matrix products, attend_back(): jnp.einsum('rqhd,rkhd->rhqk', grad_heads, split_heads(value_rows), prefer...  27.9 us
    convert_element_type x2, other arithmetic, attend_back(): grad_scores = (weights * (grad_weights - row_inner)).astype(jnp.bfloat16)  24.3 us
    dot_general x2, matrix products, attend_back(): jnp.einsum('rhqk,rqhd->rkhd', weights.astype(jnp.bfloat16), grad_heads, p...  21.8 us
    dot_general x6, matrix products, weight_grad(): jnp.einsum('rtd,rte->de', left, right, preferred_element_type=jnp.float32)  18.3 us
  transfers between devices with their start and end apart: 8, of which 5 were waited for; matrix products, arithmetic and copies ran while one was open for 24% of the time, Pallas kernels for 0%

commit v1 on v0

v1 whole, which is shorter than its diff:
```python
import functools

import jax
import jax.numpy as jnp
from jax import lax
from jax.experimental import pallas as pl
from jax.experimental.pallas import tpu as pltpu
from jax.sharding import PartitionSpec as P

HEADS = 8
SCORE_SCALE = 0.125
EPSILON = 1e-05
ROOT_HALF = 0.7071067811865476
NORMAL_DENSITY = 0.3989422804014327

BIG=float(2.0**30)
HALF=64
LSE=8; DELTA=32
NT=(((1,),(1,)),((),()))
F32=jnp.float32; BF=jnp.bfloat16
def lanes(shape): return lax.broadcasted_iota(jnp.int32,shape,len(shape)-1)
def pick(even, mine, aux):
    low=lanes(mine.shape)<HALF
    return jnp.where(low,mine,aux) if even else jnp.where(low,aux,mine)
def dot_nt(a,b): return lax.dot_general(a,b,NT,preferred_element_type=F32)
def dot_nn(a,b): return jnp.dot(a,b,preferred_element_type=F32)
def put_parts(aux,x,at):
    lane=lanes(aux.shape)%HALF
    hi=x.astype(BF).astype(F32); r=x-hi; mid=r.astype(BF).astype(F32)
    return jnp.where(lane==at,hi,jnp.where(lane==at+1,mid,jnp.where(lane==at+2,r-mid,aux)))
def row_const(shape,at,n,val):
    lane=lanes(shape)%HALF
    return (lane>=at)&(lane<at+n)
def schedule(n,ahead,first,rest):
    kept={}
    for h in range(min(ahead,n)): kept[h]=first(h)
    for h in range(n):
        if h+ahead<n: kept[h+ahead]=first(h+ahead)
        rest(h,kept.pop(h))

def fwd_kernel(tq,width,causal,ahead,start_ref,count_ref,base_ref,q_ref,aq_ref,k_ref,v_ref,ak_ref,o_ref,l_ref):
    rows=q_ref.shape[0]; subs=q_ref.shape[1]//tq; keys=k_ref.shape[1]; heads=q_ref.shape[2]//HALF
    def step(i,_):
        r=i//subs; s=i%subs
        n=count_ref[r,s]; st=pl.multiple_of(start_ref[r,s],128)
        qs=pl.ds(pl.multiple_of(s*tq,tq),tq)
        for blocks in range(1,keys//width+1):
            @pl.when(n==blocks)
            def _(blocks=blocks):
                span=blocks*width
                ks=pl.ds(st,span)
                ak=ak_ref[r,ks]; aq=aq_ref[r,qs]
                state={"stats":aq.astype(F32)}
                if causal:
                    qp=base_ref[0]+s*tq+lax.broadcasted_iota(jnp.int32,(tq,width),0)
                    kp=st+span-width+lax.broadcasted_iota(jnp.int32,(tq,width),1)
                    seen=kp<=qp
                def first(h):
                    cs=slice(h//2*128,h//2*128+128)
                    q=q_ref[r,qs,cs]*jnp.asarray(0.125,BF); k=k_ref[r,ks,cs]
                    return dot_nt(pick(h%2==0,q,aq),pick(h%2==0,k,ak))
                def rest(h,S):
                    cs=slice(h//2*128,h//2*128+128)
                    v=v_ref[r,ks,cs]
                    if causal:
                        tail=jnp.where(seen,S[:,span-width:],-BIG)
                        S=tail if blocks==1 else jnp.concatenate([S[:,:span-width],tail],axis=1)
                    m=jnp.max(S,axis=1,keepdims=True)
                    W=jnp.exp(S-m).astype(BF)
                    R=dot_nn(W,pick(h%2==0,v,jnp.ones_like(v)))
                    at=64 if h%2==0 else 0
                    state["stats"]=put_parts(state["stats"],m+jnp.log(R[:,at:at+1]),LSE+3*h)
                    if h%2==0: state["even"]=R
                    else:
                        low=lanes((tq,128))<HALF
                        total=pltpu.roll(jnp.where(low,R,state["even"]),HALF,1)
                        o_ref[r,qs,cs]=(jnp.where(low,state["even"],R)/total).astype(o_ref.dtype)
                schedule(heads,ahead,first,rest)
                l_ref[r,qs]=state["stats"].astype(BF)
        return 0
    lax.fori_loop(0,rows*subs,step,0)

def bwd_kernel(dkv,tq,width,causal,ahead,start_ref,count_ref,base_ref,a_ref,b_ref,aq_ref,ak_ref,k_ref,v_ref,*outs):
    loc=k_ref if dkv else a_ref
    win=a_ref if dkv else k_ref
    rows=loc.shape[0]; subs=loc.shape[1]//tq; keys=win.shape[1]; heads=loc.shape[2]//HALF
    def step(i,_):
        r=i//subs; s=i%subs
        n=count_ref[r,s]; st=pl.multiple_of(start_ref[r,s],128)
        ls=pl.ds(pl.multiple_of(s*tq,tq),tq)
        if dkv:
            @pl.when(n==0)
            def _():
                for out in outs: out[r,ls]=jnp.zeros((tq,out.shape[2]),out.dtype)
        for blocks in range(1,keys//width+1):
            @pl.when(n==blocks)
            def _(blocks=blocks):
                span=blocks*width
                ws=pl.ds(st,span)
                qs,ks=(ws,ls) if dkv else (ls,ws)
                ak=ak_ref[r,ks]; aq=aq_ref[r,qs]
                state={}
                if causal:
                    at=base_ref[0]+s*tq
                    if dkv:
                        seen=at+lax.broadcasted_iota(jnp.int32,(tq,width),0)<=st+lax.broadcasted_iota(jnp.int32,(tq,width),1)
                    else:
                        seen=st+span-width+lax.broadcasted_iota(jnp.int32,(tq,width),1)<=at+lax.broadcasted_iota(jnp.int32,(tq,width),0)
                minus=jnp.asarray(-1.0,BF)
                def first(h):
                    e=h%2==0
                    cs=slice(h//2*128,h//2*128+128)
                    q=a_ref[r,qs,cs]*jnp.asarray(0.125,BF); g=b_ref[r,qs,cs]; k=k_ref[r,ks,cs]; v=v_ref[r,ks,cs]
                    ka=pick(e,k,jnp.where(row_const(ak.shape,LSE+3*h,3,-1),minus,ak))
                    va=pick(e,v,jnp.where(row_const(v.shape,DELTA+3*h,3,-1),minus,jnp.zeros_like(v)))
                    qa=pick(e,q,aq); ga=pick(e,g,aq)
                    if dkv: return dot_nt(ka,qa),dot_nt(va,ga)
                    return dot_nt(qa,ka),dot_nt(ga,va)
                def rest(h,XG):
                    X,G=XG
                    cs=slice(h//2*128,h//2*128+128)
                    if causal:
                        if dkv:
                            X1=jnp.where(seen,X[:,:width],-BIG)
                            X=X1 if blocks==1 else jnp.concatenate([X1,X[:,width:]],axis=1)
                        else:
                            X1=jnp.where(seen,X[:,span-width:],-BIG)
                            X=X1 if blocks==1 else jnp.concatenate([X[:,:span-width],X1],axis=1)
                    W=jnp.exp(X); D=(W*G).astype(BF)
                    low=lanes((tq,128))<HALF
                    if not dkv:
                        R=dot_nn(D,k_ref[r,ks,cs])
                        if h%2==0: state["a"]=R
                        else: outs[0][r,ls,cs]=(0.125*jnp.where(low,state["a"],R)).astype(outs[0].dtype)
                    else:
                        R2=dot_nn(W.astype(BF),b_ref[r,qs,cs])
                        R=dot_nn(D,a_ref[r,qs,cs])
                        if h%2==0: state["a"]=R; state["b"]=R2
                        else:
                            outs[0][r,ls,cs]=(0.125*jnp.where(low,state["a"],R)).astype(outs[0].dtype)
                            outs[1][r,ls,cs]=jnp.where(low,state["b"],R2).astype(outs[1].dtype)
                schedule(heads,ahead,first,rest)
        return 0
    lax.fori_loop(0,rows*subs,step,0)
SM=pl.BlockSpec(memory_space=pltpu.SMEM); VM=pl.BlockSpec(memory_space=pltpu.VMEM)
def fwd(tq,width,causal,ahead,start,count,base,q,aq,k,v,ak):
    R,T,D=q.shape
    return pl.pallas_call(functools.partial(fwd_kernel,tq,width,causal,ahead),
        out_shape=(jax.ShapeDtypeStruct(q.shape,BF),jax.ShapeDtypeStruct((R,T,128),BF)),
        in_specs=[SM]*3+[VM]*5,out_specs=(VM,VM),name="attend_rows",
        compiler_params=pltpu.CompilerParams(vmem_limit_bytes=48<<20))(start,count,base,q,aq,k,v,ak)
def bwd_dq(tq,width,causal,ahead,start,count,base,q,g,aq,ak,k,v):
    return pl.pallas_call(functools.partial(bwd_kernel,False,tq,width,causal,ahead),
        out_shape=(jax.ShapeDtypeStruct(q.shape,BF),),
        in_specs=[SM]*3+[VM]*6,out_specs=(VM,),name="query_grad",
        compiler_params=pltpu.CompilerParams(vmem_limit_bytes=48<<20))(start,count,base,q,g,aq,ak,k,v)[0]
def bwd_dkv(tq,width,causal,ahead,start,count,base,q,g,aq,ak,k,v):
    return pl.pallas_call(functools.partial(bwd_kernel,True,tq,width,causal,ahead),
        out_shape=(jax.ShapeDtypeStruct(k.shape,BF),)*2,
        in_specs=[SM]*3+[VM]*6,out_specs=(VM,VM),name="key_grad",
        compiler_params=pltpu.CompilerParams(vmem_limit_bytes=48<<20))(start,count,base,q,g,aq,ak,k,v)
def aux_q(seg):
    lane=jnp.arange(128)%HALF
    return jnp.where((lane<8)&(seg[...,None]==lane),1.0,0.0).astype(BF)
def aux_k(seg,valid=None):
    lane=jnp.arange(128)%HALF
    ok=seg[...,None]==lane
    if valid is not None: ok=ok&valid[...,None]
    return jnp.where((lane<8)&~ok,-BIG,0.0).astype(BF)

def gather_row(block, axis=1):
    size = lax.axis_size("seq")
    place = lax.axis_index("seq")
    held = {0: block}
    bit = size // 2
    while bit:
        swap = [(i, i ^ bit) for i in range(size)]
        for key in list(held):
            held[key | bit] = lax.ppermute(held[key], "seq", swap)
        bit //= 2
    shape = list(block.shape)
    extent = shape[axis]
    shape[axis] = extent * size
    full = jnp.zeros(shape, block.dtype)
    for key, value in held.items():
        at = [0] * len(shape)
        at[axis] = (place ^ key) * extent
        full = lax.dynamic_update_slice(full, value, at)
    return full


def count_below(ids, bound):
    return jnp.sum((ids[:, None, :] < bound[:, :, None]).astype(jnp.int32), axis=-1)


def window(low, high, width, extent):
    floor = low // 128 * 128
    blocks = jnp.where(high > low, (high - floor + width - 1) // width, 0)
    start = jnp.minimum(floor, extent - blocks * width)
    return start.astype(jnp.int32), blocks.astype(jnp.int32)


def with_inner(aux, grad_mixed, mixed):
    width = mixed.shape[-1]
    lane = jnp.arange(128) % HALF
    head = (lane - DELTA) // 3
    chosen = (
        (jnp.arange(width)[:, None] // HALF == head[None]) & (lane >= DELTA) & (lane < DELTA + 3 * HEADS)
    ).astype(F32)
    inner = jnp.einsum(
        "rtd,dl->rtl",
        grad_mixed.astype(F32) * mixed.astype(F32),
        chosen,
        precision=lax.Precision.HIGHEST,
        preferred_element_type=F32,
    )
    high = lax.reduce_precision(inner, 8, 7)
    rest = inner - high
    middle = lax.reduce_precision(rest, 8, 7)
    part = (lane - DELTA) % 3
    return (
        aux.astype(F32) + jnp.where(part == 0, high, jnp.where(part == 1, middle, rest - middle))
    ).astype(BF)

def project(values, weight):
    return jnp.einsum("rtd,de->rte", values, weight, preferred_element_type=jnp.float32)


def weight_grad(left, right):
    return jnp.einsum("rtd,rte->de", left, right, preferred_element_type=jnp.float32)


def input_grad(grad, weight):
    return jnp.einsum("rte,de->rtd", grad, weight, preferred_element_type=jnp.float32)


def token_sum(values):
    return jnp.sum(values.astype(jnp.float32), axis=(0, 1))


def gelu_slope(values):
    return 0.5 * (1.0 + lax.erf(values * ROOT_HALF)) + values * NORMAL_DENSITY * jnp.exp(
        -0.5 * values * values
    )


def normalize(residual, gain, shift):
    centred = residual - jnp.mean(residual, axis=-1, keepdims=True)
    inverse_root = lax.rsqrt(jnp.mean(centred * centred, axis=-1, keepdims=True) + EPSILON)
    unit_rows = centred * inverse_root
    return (unit_rows * gain + shift, unit_rows, inverse_root)


def normalize_back(grad, unit_rows, inverse_root, gain):
    scaled = grad * gain
    grad_residual = inverse_root * (
        scaled
        - jnp.mean(scaled, axis=-1, keepdims=True)
        - unit_rows * jnp.mean(scaled * unit_rows, axis=-1, keepdims=True)
    )
    return (grad_residual, jnp.sum(grad * unit_rows, axis=(0, 1)), jnp.sum(grad, axis=(0, 1)))


def shards(
    tokens,
    memory,
    segment_ids,
    source_ids,
    source_lengths,
    cotangent,
    self_qkv,
    self_out,
    cross_q,
    cross_kv,
    cross_out,
    ffn_in,
    ffn_out,
    norm_gains,
    bias_rows,
    hidden_bias,
):
    model_width = tokens.shape[2]
    local_len = tokens.shape[1]
    seq_place = lax.axis_index("seq")
    base = (seq_place * local_len).astype(jnp.int32)
    rows = tokens.shape[0]
    base_ref = base.reshape((1,))
    tokens_full = gather_row(tokens)
    row_ids = gather_row(jnp.stack([segment_ids, source_ids]), axis=2)
    memory_full = gather_row(memory)
    row_segments, row_sources = row_ids[0], row_ids[1]
    row_len, source_len = row_segments.shape[1], row_sources.shape[1]
    source_pos = jnp.arange(source_len, dtype=jnp.int32)
    usable = source_pos[None] < source_lengths[:, None]
    masked_sources = jnp.where(usable, row_sources, 1 << 20)
    local_pos = base + jnp.arange(local_len, dtype=jnp.int32)
    local_usable = local_pos[None] < source_lengths[:, None]
    aux_query = aux_q(segment_ids)
    aux_key = aux_k(row_segments)
    aux_key_local = aux_k(segment_ids)
    aux_source = aux_k(row_sources, usable)
    aux_source_local = aux_k(source_ids, local_usable)

    wide = 256
    first_seg, last_seg = segment_ids[:, ::wide], segment_ids[:, wide - 1 :: wide]
    tops = base + jnp.arange(0, local_len, wide, dtype=jnp.int32)[None] + jnp.zeros((rows, 1), jnp.int32)
    low = count_below(row_segments, first_seg) // wide * wide
    self_start, self_count = window(low, tops + wide, wide, row_len)
    back_start, back_count = window(tops, count_below(row_segments, last_seg + 1), wide, row_len)
    fine = 128
    cross_start, cross_count = window(
        count_below(masked_sources, segment_ids[:, ::fine]),
        count_below(masked_sources, segment_ids[:, fine - 1 :: fine] + 1),
        wide,
        source_len,
    )
    source_tops = base + jnp.arange(0, local_len, fine, dtype=jnp.int32)[None]
    source_last = jnp.clip(source_lengths[:, None] - 1 - base, 0, local_len - 1)
    last_index = jnp.minimum(source_tops - base + fine - 1, source_last)
    source_high = jnp.take_along_axis(source_ids, last_index, axis=1)
    source_high = jnp.where(source_tops < source_lengths[:, None], source_high, -1)
    feed_start, feed_count = window(
        count_below(row_segments, source_ids[:, ::fine]),
        count_below(row_segments, source_high + 1),
        wide,
        row_len,
    )

    projected = project(tokens_full, self_qkv)
    queries_full = (projected[:, :, :model_width] + bias_rows[3]).astype(BF)
    key_full = projected[:, :, model_width : 2 * model_width].astype(BF)
    value_full = (projected[:, :, 2 * model_width :] + bias_rows[4]).astype(BF)
    local = lambda array: lax.dynamic_slice_in_dim(array, base, local_len, 1)
    queries = local(queries_full)
    attended, self_aux = fwd(
        wide, wide, True, 1, self_start, self_count, base_ref, queries, aux_query, key_full, value_full, aux_key
    )
    after_self, unit_first, root_first = normalize(
        tokens.astype(jnp.float32) + project(attended, self_out) + bias_rows[5],
        norm_gains[0],
        bias_rows[0],
    )
    self_low = after_self.astype(jnp.bfloat16)
    cross_query = (project(self_low, cross_q) + bias_rows[6]).astype(jnp.bfloat16)
    cross_query_full = gather_row(cross_query)
    key_value = project(memory_full, cross_kv)
    cross_key = key_value[:, :, :model_width].astype(BF)
    cross_value = (key_value[:, :, model_width:] + bias_rows[7]).astype(BF)
    crossed, cross_aux = fwd(
        fine, wide, False, 2, cross_start, cross_count, base_ref, cross_query, aux_query, cross_key, cross_value, aux_source
    )
    after_cross, unit_second, root_second = normalize(
        after_self + project(crossed, cross_out) + bias_rows[8], norm_gains[1], bias_rows[1]
    )
    cross_low = after_cross.astype(jnp.bfloat16)
    before = project(cross_low, ffn_in) + hidden_bias
    hidden = jax.nn.gelu(before, approximate=False).astype(jnp.bfloat16)
    output, unit_third, root_third = normalize(
        after_cross + project(hidden, ffn_out) + bias_rows[9], norm_gains[2], bias_rows[2]
    )
    grad_third, gain_third, shift_third = normalize_back(
        cotangent.astype(jnp.float32), unit_third, root_third, norm_gains[2]
    )
    ffn_branch = grad_third.astype(jnp.bfloat16)
    bias_ffn_out = token_sum(ffn_branch)
    grad_ffn_out = weight_grad(hidden, ffn_branch)
    grad_hidden = (input_grad(ffn_branch, ffn_out) * gelu_slope(before)).astype(jnp.bfloat16)
    grad_hbias = token_sum(grad_hidden)
    grad_ffn_in = weight_grad(cross_low, grad_hidden)
    grad_second = grad_third + input_grad(grad_hidden, ffn_in)
    grad_mid, gain_second, shift_second = normalize_back(
        grad_second, unit_second, root_second, norm_gains[1]
    )
    cross_branch = grad_mid.astype(jnp.bfloat16)
    bias_cross_out = token_sum(cross_branch)
    grad_cross_out = weight_grad(crossed, cross_branch)
    grad_crossed = input_grad(cross_branch, cross_out).astype(jnp.bfloat16)
    grad_crossed_full = gather_row(grad_crossed)
    cross_aux = with_inner(cross_aux, grad_crossed, crossed)
    cross_aux_full = gather_row(cross_aux)
    grad_cquery = bwd_dq(
        fine, wide, False, 2, cross_start, cross_count, base_ref, cross_query, grad_crossed, cross_aux, aux_source, cross_key, cross_value
    )
    bias_cross_query = token_sum(grad_cquery)
    grad_cross_q = weight_grad(self_low, grad_cquery)
    grad_first = grad_mid + input_grad(grad_cquery, cross_q)
    grad_start, gain_first, shift_first = normalize_back(
        grad_first, unit_first, root_first, norm_gains[0]
    )
    self_branch = grad_start.astype(jnp.bfloat16)
    bias_self_out = token_sum(self_branch)
    grad_self_out = weight_grad(attended, self_branch)
    grad_attended = input_grad(self_branch, self_out).astype(jnp.bfloat16)
    grad_attended_full = gather_row(grad_attended)
    self_aux = with_inner(self_aux, grad_attended, attended)
    self_aux_full = gather_row(self_aux)
    grad_ckey, grad_cvalue = bwd_dkv(
        fine, wide, False, 2, feed_start, feed_count, base_ref, cross_query_full, grad_crossed_full, cross_aux_full, aux_source_local,
        local(cross_key), local(cross_value)
    )
    grad_pair = jnp.concatenate([grad_ckey, grad_cvalue], axis=2)
    bias_cross_value = token_sum(grad_cvalue)
    grad_cross_kv = weight_grad(memory, grad_pair)
    grad_memory = input_grad(grad_pair, cross_kv).astype(jnp.bfloat16)
    grad_query = bwd_dq(
        wide, wide, True, 1, self_start, self_count, base_ref, queries, grad_attended, self_aux, aux_key, key_full, value_full
    )
    grad_key, grad_value = bwd_dkv(
        wide, wide, True, 1, back_start, back_count, base_ref, queries_full, grad_attended_full, self_aux_full, aux_key_local,
        local(key_full), local(value_full)
    )
    joined = jnp.concatenate([grad_query, grad_key, grad_value], axis=2)
    bias_query = token_sum(grad_query)
    bias_value = token_sum(grad_value)
    grad_self_qkv = weight_grad(tokens, joined)
    grad_tokens = (grad_start + input_grad(joined, self_qkv)).astype(jnp.bfloat16)
    reduced = lax.psum(
        (
            grad_self_qkv,
            grad_self_out,
            grad_cross_q,
            grad_cross_kv,
            grad_cross_out,
            grad_ffn_in,
            grad_ffn_out,
            jnp.stack([gain_first, gain_second, gain_third]),
            jnp.stack(
                [
                    shift_first,
                    shift_second,
                    shift_third,
                    bias_query,
                    bias_value,
                    bias_self_out,
                    bias_cross_query,
                    bias_cross_value,
                    bias_cross_out,
                    bias_ffn_out,
                ]
            ),
            grad_hbias,
        ),
        ("dp", "seq"),
    )
    return (
        output.astype(jnp.bfloat16),
        grad_tokens,
        grad_memory,
        reduced[0],
        reduced[1],
        reduced[2],
        reduced[3],
        reduced[4],
        reduced[5],
        reduced[6],
        reduced[7],
        reduced[8],
        reduced[9],
    )


def solution(mesh):
    placed = (
        P("dp", "seq", None),
        P("dp", "seq", None),
        P("dp", "seq"),
        P("dp", "seq"),
        P("dp"),
        P("dp", "seq", None),
        P(),
        P(),
        P(),
        P(),
        P(),
        P(),
        P(),
        P(),
        P(),
        P(),
    )
    return jax.shard_map(
        shards,
        mesh=mesh,
        in_specs=placed,
        out_specs=(
            P("dp", "seq", None),
            P("dp", "seq", None),
            P("dp", "seq", None),
            P(),
            P(),
            P(),
            P(),
            P(),
            P(),
            P(),
            P(),
            P(),
            P(),
        ),
        check_vma=False,
    )
```

time: 627 us -> 534 us (0.85)
  matrix products: 143 us -> 53 us
  Pallas kernels: 0 us -> 43.2 us
  waiting for transfers between devices: 285 us -> 253 us
  other arithmetic: 57 us -> 36.6 us
  starting transfers between devices: 0.79 us -> 17.8 us
  local copies, waits for them, and re-layouts: 64.6 us -> 54 us
    dot_general x14 -> x2, matrix products: 100 us -> 1.71 us  [with_inner(): jnp.einsum('rtd,dl->rtl', grad_mixed.astype(F32) * mixed.astype(F32), cho...]
    pallas_call x0 -> x6, Pallas kernels: none -> 43.2 us  [the longest x2 15.8 us: fwd(): pl.pallas_call(functools.partial(fwd_kernel, tq, width, causal, ahead), o...]
    reduce_scatter x4 -> x0, waiting for transfers between devices: 29.4 us -> none  [the longest x1 29.4 us: shards(): lax.psum_scatter(grad_key.astype(jnp.bfloat16), 'seq', scatter_dimension=...]
    convert_element_type x6 -> x4, other arithmetic: 30.8 us -> 7.84 us  [the longest x1 4.66 us: shards(): value_full = (projected[:, :, 2 * model_width:] + bias_rows[4]).astype(BF)]
    ppermute x0 -> x24, waiting for transfers between devices: none -> 21.3 us  [gather_row(): held[key | bit] = lax.ppermute(held[key], 'seq', swap)]
    all_gather x3 -> x0, waiting for transfers between devices: 20.4 us -> none  [the longest x1 8.25 us: shards(): lax.all_gather(key_rows, 'seq', axis=1, tiled=True)]
    convert_element_type x9 -> x0, local copies, waits for them, and re-layouts: 19.5 us -> none  [the longest x1 4.08 us: shards(): grad_key.astype(jnp.bfloat16)]
    ppermute x0 -> x24, starting transfers between devices: none -> 17.7 us  [gather_row(): held[key | bit] = lax.ppermute(held[key], 'seq', swap)]
  transfers between devices with their start and end apart: 8 -> 25, of which waited for: 5 -> 6; matrix products, arithmetic and copies ran while one was open for 24% -> 19% of each run, Pallas kernels for 0% -> 5%
where the time goes in v1:
time: 534 us; the launch traced here: 525 us
  waiting for transfers between devices  253 us (47%)
  local copies, waits for them, and re-layouts  54 us (10%)
  matrix products  53 us (10%)
  blocking collectives  51.8 us (10%)
  Pallas kernels  43.2 us (8%)
  other arithmetic  36.6 us (7%)
  starting transfers between devices  17.8 us (3%)
  between operations  15.7 us (3%)
    psum x1, waiting for transfers between devices, shards(): lax.psum((grad_self_qkv, grad_self_out, grad_cross_q, grad_cross_kv, grad...  232 us
    psum x1, blocking collectives, shards(): lax.psum((grad_self_qkv, grad_self_out, grad_cross_q, grad_cross_kv, grad...  51.8 us
    unnamed x190, local copies, waits for them, and re-layouts  22.3 us
    ppermute x24, waiting for transfers between devices, gather_row(): held[key | bit] = lax.ppermute(held[key], 'seq', swap)  21.3 us
    ppermute x24, starting transfers between devices, gather_row(): held[key | bit] = lax.ppermute(held[key], 'seq', swap)  17.7 us
    dot_general x7, matrix products, project(): jnp.einsum('rtd,de->rte', values, weight, preferred_element_type=jnp.floa...  17.7 us
    dot_general x7, matrix products, weight_grad(): jnp.einsum('rtd,rte->de', left, right, preferred_element_type=jnp.float32)  17.2 us
    dot_general x7, matrix products, input_grad(): jnp.einsum('rte,de->rtd', grad, weight, preferred_element_type=jnp.float32)  16.5 us
  transfers between devices with their start and end apart: 25, of which 6 were waited for; matrix products, arithmetic and copies ran while one was open for 19% of the time, Pallas kernels for 5%

profile of v1, /device:TPU:0, one launch (start us, length us, event | category | flops | bytes accessed | tf_op | source)
XLA Modules:
  0.0 525.3 jit_solution(6174774001535750618)
XLA Ops:
  8.1 3.0 collective-permute-start
  34.3 2.3 select_convert_fusion
  51.0 3.9 fusion.54
  57.6 6.3 %fusion.26 = f32[2,1024,1536]{2,1,0:T(8,128)} fusion(bf16[2,1024,512]{2,1,0:T(8,128)(2,1)S(1)} %constant_dynamic-update-slice_fusion.24, bf16[512,1536]{1,0:T(8,128)(2,1)S(1)} %copy-done.78), kind=kOutput, calls=%fused_computation.52 | convolution fusion | flops 3221225472 | bytes 16252928 | tf_op jit(solution)/shard_map/rtd,de->rte/dot_general | solution.py:226
  64.0 2.5 slice.139.k_ref
  66.5 4.7 fusion.9
  71.2 8.3 %attend_rows.2 = (bf16[2,256,512]{2,1,0:T(8,128)(2,1)S(1)}, bf16[2,256,128]{2,1,0:T(8,128)(2,1)S(1)}) custom-call(s32[2,1]{1,0:T(2,128)S(1)} %get-tuple-element.110.start_ref, s32[2,1]{1,0:T(2,128)S(1)} %get-tuple-element.111.count_ref, s32[1]{0:T(128)} %bitcast.4.base_ref, bf16[2,256,512]{2,1,0:T(8,128)(2,1)S(1)} %constant_dynamic-slice_fusion.4.q_ref.a_ref, ...), custom_call_target="tpu_custom_call" | custom-call | tf_op jit(solution)/shard_map/attend_rows/pallas_call | solution.py:148
  85.5 7.6 %attend_rows.3 = (bf16[2,256,512]{2,1,0:T(8,128)(2,1)S(1)}, bf16[2,256,128]{2,1,0:T(8,128)(2,1)S(1)}) custom-call(s32[2,2]{1,0:T(2,128)S(1)} %get-tuple-element.114.start_ref, s32[2,2]{1,0:T(2,128)S(1)} %get-tuple-element.115.count_ref, s32[1]{0:T(128)} %bitcast.4.base_ref, bf16[2,256,512]{2,1,0:T(8,128)(2,1)S(1)} %get-tuple-element.155.q_ref.a_ref, ...), custom_call_target="tpu_custom_call" | custom-call | tf_op jit(solution)/shard_map/attend_rows/pallas_call | solution.py:148
  94.1 2.5 fusion.65
  96.6 10.2 %fusion.2 = bf16[2,256,2048]{2,1,0:T(8,128)(2,1)S(1)} fusion(f32[2,256,2048]{2,1,0:T(8,128)S(1)} %get-tuple-element.145, f32[2048]{0:T(1024)S(1)} %copy-done.66, u8[256,2048]{1,0:T(8,128)(4,1)S(1)} %get-tuple-element.69, u8[256,2048]{1,0:T(8,128)(4,1)S(1)} %get-tuple-element.68), kind=kLoop, calls=%fused_computation.5 | loop fusion | flops 74448896 | bytes 7348224 | tf_op jit(solution)/shard_map/convert_element_type | solution.py:357
  111.6 3.3 convert_reduce_fusion
  114.8 2.3 multiply_reduce_fusion
  121.6 7.5 %query_grad.2 = bf16[2,256,512]{2,1,0:T(8,128)(2,1)S(1)} custom-call(s32[2,2]{1,0:T(2,128)S(1)} %get-tuple-element.114.start_ref, s32[2,2]{1,0:T(2,128)S(1)} %get-tuple-element.115.count_ref, s32[1]{0:T(128)} %bitcast.4.base_ref, bf16[2,256,512]{2,1,0:T(8,128)(2,1)S(1)} %get-tuple-element.155.q_ref.a_ref, bf16[2,256,512]{2,1,0:T(8,128)(2,1)S(1)} %get-tuple-element.157.b_ref, ...), custom_call_target="tpu_custom_call" | custom-call | tf_op jit(solution)/shard_map/query_grad/pallas_call | solution.py:153
  129.3 2.9 multiply_reduce_fusion.1
  134.0 3.5 convolution_bitcast_fusion.1
  137.4 3.3 convolution_bitcast_fusion
  146.0 4.3 query_grad.3
  150.3 4.7 collective-permute-start.12
  155.0 2.2 collective-permute-start.13
  163.6 18.7 %collective-permute-done.18 = bf16[2,256,512]{2,1,0:T(8,128)(2,1)S(1)} collective-permute-done((bf16[2,256,512]{2,1,0:T(8,128)(2,1)S(1)}, bf16[2,256,512]{2,1,0:T(8,128)(2,1)S(1)}, u32[]{:S(2)}, u32[]{:S(2)}) %collective-permute-start.18) | collective-permute-done | bytes 524320 | tf_op jit(solution)/shard_map/ppermute | solution.py:179
  186.8 6.1 %key_grad.3 = (bf16[2,256,512]{2,1,0:T(8,128)(2,1)S(1)}, bf16[2,256,512]{2,1,0:T(8,128)(2,1)S(1)}) custom-call(s32[2,2]{1,0:T(2,128)S(1)} %copy-done.7, s32[2,2]{1,0:T(2,128)S(1)} %copy-done.8, s32[1]{0:T(128)} %bitcast.4.base_ref, bf16[2,1024,512]{2,1,0:T(8,128)(2,1)} %constant_dynamic-update-slice_fusion.8.a_ref, bf16[2,1024,512]{2,1,0:T(8,128)(2,1)} %copy-done.14, ...), custom_call_target="tpu_custom_call" | custom-call | tf_op jit(solution)/shard_map/key_grad/pallas_call | solution.py:158
  193.1 2.1 convolution_bitcast_fusion.3
  196.0 9.5 %key_grad.2 = (bf16[2,256,512]{2,1,0:T(8,128)(2,1)S(1)}, bf16[2,256,512]{2,1,0:T(8,128)(2,1)S(1)}) custom-call(s32[2,1]{1,0:T(2,128)S(1)} %get-tuple-element.108.start_ref, s32[2,1]{1,0:T(2,128)S(1)} %get-tuple-element.109.count_ref, s32[1]{0:T(128)} %bitcast.4.base_ref, bf16[2,1024,512]{2,1,0:T(8,128)(2,1)S(1)} %copy-done.5, ...), custom_call_target="tpu_custom_call" | custom-call | tf_op jit(solution)/shard_map/key_grad/pallas_call | solution.py:158
  205.5 3.7 convolution_bitcast_fusion.2
  210.6 51.8 %all-reduce = (f32[3,512]{1,0:T(4,128)}, f32[10,512]{1,0:T(8,128)}, f32[2048]{0:T(1024)}) all-reduce(f32[3,512]{1,0:T(4,128)S(1)} %pad_maximum_fusion.3, f32[10,512]{1,0:T(8,128)S(1)} %stack.71, f32[2048]{0:T(1024)S(1)} %copy-done.63), channel_id=1, replica_groups=mesh['dp'=8,'seq'=4] {'dp','seq'}, use_global_device_ids=true, to_apply=%region_28.29 | all-reduce | flops 8704 | bytes 69632 | tf_op jit(solution)/shard_map/psum | solution.py:417
  262.3 3.2 convolution_convert_fusion.2
  265.5 3.8 fusion.45
  269.3 232.1 %all-reduce.4.cloned.1.call-done = (f32[512,1536]{0,1:T(8,128)}, f32[512,512]{1,0:T(8,128)}, f32[512,512]{1,0:T(8,128)}, f32[512,1024]{0,1:T(8,128)}, f32[512,51...) async-done(((f32[512,1536]{0,1:T(8,128)}, f32[512,512]{1,0:T(8,128)}, f32[512,512]{1,0:T(8,128)}, f32[512,1024]{0,1:T(8,128)}, f32[512,512]{1,0:T(8,128)}, ...) | async-done | bytes 16777232 | tf_op jit(solution)/shard_map/psum | solution.py:417
  501.4 3.7 copy.81
  506.9 2.4 copy.130
  509.3 2.3 copy.131
  512.6 2.1 copy.133
  (347 shorter events, 83.1 us)
Async XLA Ops:
  7.2 86.9 %copy-start = (bf16[512,2048]{1,0:T(8,128)(2,1)S(1)}, bf16[512,2048]{1,0:T(8,128)(2,1)}, u32[]{:S(2)}) copy-start(bf16[512,2048]{1,0:T(8,128)(2,1)} %param.27) | copy-start | bytes 6291460
  7.2 494.2 %all-reduce.4.cloned.1.call-start = ((), (), s32[]{:S(2)}) async-start(), calls=%async_computation | async-start | bytes 33554432 | tf_op jit(solution)/shard_map/psum | solution.py:417
  8.1 21.6 %collective-permute-start = (s32[2,2,256]{2,1,0:T(2,128)S(1)}, s32[2,2,256]{2,1,0:T(2,128)S(1)}, u32[]{:S(2)}, u32[]{:S(2)}) collective-permute-start(s32[2,2,256]{2,1,0:T(2,128)S(1)} %get-tuple-element.134), channel_id=1, source_target_pairs={{0,2},{1,3},{2,0},{3,1},{4,6},{5,7},{6,4},{7,5},{8,10},{9,11},{10,... | collective-permute-start | bytes 12296 | tf_op jit(solution)/shard_map/ppermute | solution.py:179
  11.1 18.7 %collective-permute-start.1 = (s32[2,2,256]{2,1,0:T(2,128)S(1)}, s32[2,2,256]{2,1,0:T(2,128)S(1)}, u32[]{:S(2)}, u32[]{:S(2)}) collective-permute-start(s32[2,2,256]{2,1,0:T(2,128)S(1)} %get-tuple-element.134), channel_id=1, source_target_pairs={{0,1},{1,0},{2,3},{3,2},{4,5},{5,4},{6,7},{7,6},{8,9},{9,8},{10,11... | collective-permute-start | bytes 12296 | tf_op jit(solution)/shard_map/ppermute | solution.py:179
  11.1 30.3 %collective-permute-start.6 = (bf16[2,256,512]{2,1,0:T(8,128)(2,1)}, bf16[2,256,512]{2,1,0:T(8,128)(2,1)}, u32[]{:S(2)}, u32[]{:S(2)}) collective-permute-start(bf16[2,256,512]{2,1,0:T(8,128)(2,1)} %param.17), channel_id=1, source_target_pairs={{0,2},{1,3},{2,0},{3,1},{4,6},{5,7},{6,4},{7,5},{8,10},{9,11},{10,... | collective-permute-start | bytes 1572872 | tf_op jit(solution)/shard_map/ppermute | solution.py:179
  11.2 35.2 %collective-permute-start.7 = (bf16[2,256,512]{2,1,0:T(8,128)(2,1)}, bf16[2,256,512]{2,1,0:T(8,128)(2,1)}, u32[]{:S(2)}, u32[]{:S(2)}) collective-permute-start(bf16[2,256,512]{2,1,0:T(8,128)(2,1)} %param.17), channel_id=1, source_target_pairs={{0,1},{1,0},{2,3},{3,2},{4,5},{5,4},{6,7},{7,6},{8,9},{9,8},{10,11... | collective-permute-start | bytes 1572872 | tf_op jit(solution)/shard_map/ppermute | solution.py:179
  11.6 30.7 %collective-permute-start.3 = (bf16[2,256,512]{2,1,0:T(8,128)(2,1)}, bf16[2,256,512]{2,1,0:T(8,128)(2,1)}, u32[]{:S(2)}, u32[]{:S(2)}) collective-permute-start(bf16[2,256,512]{2,1,0:T(8,128)(2,1)} %param.16), channel_id=1, source_target_pairs={{0,2},{1,3},{2,0},{3,1},{4,6},{5,7},{6,4},{7,5},{8,10},{9,11},{10,... | collective-permute-start | bytes 1572872 | tf_op jit(solution)/shard_map/ppermute | solution.py:179
  29.8 18.6 %collective-permute-start.4 = (bf16[2,256,512]{2,1,0:T(8,128)(2,1)}, bf16[2,256,512]{2,1,0:T(8,128)(2,1)}, u32[]{:S(2)}, u32[]{:S(2)}) collective-permute-start(bf16[2,256,512]{2,1,0:T(8,128)(2,1)} %param.16), channel_id=1, source_target_pairs={{0,1},{1,0},{2,3},{3,2},{4,5},{5,4},{6,7},{7,6},{8,9},{9,8},{10,11... | collective-permute-start | bytes 1572872 | tf_op jit(solution)/shard_map/ppermute | solution.py:179
  29.8 1.9 collective-permute-start.2
  41.4 8.8 %collective-permute-start.8 = (bf16[2,256,512]{2,1,0:T(8,128)(2,1)}, bf16[2,256,512]{2,1,0:T(8,128)(2,1)S(1)}, u32[]{:S(2)}, u32[]{:S(2)}) collective-permute-start(bf16[2,256,512]{2,1,0:T(8,128)(2,1)} %collective-permute-done.6), channel_id=1, source_target_pairs={{0,1},{1,0},{2,3},{3,2},{4,5},{5,4},{6,7},{7,6},{8,9},{9,8},{10,11... | collective-permute-start | bytes 1572872 | tf_op jit(solution)/shard_map/ppermute | solution.py:179
  42.4 13.9 %collective-permute-start.5 = (bf16[2,256,512]{2,1,0:T(8,128)(2,1)}, bf16[2,256,512]{2,1,0:T(8,128)(2,1)S(1)}, u32[]{:S(2)}, u32[]{:S(2)}) collective-permute-start(bf16[2,256,512]{2,1,0:T(8,128)(2,1)} %collective-permute-done.3), channel_id=1, source_target_pairs={{0,1},{1,0},{2,3},{3,2},{4,5},{5,4},{6,7},{7,6},{8,9},{9,8},{10,11... | collective-permute-start | bytes 1572872 | tf_op jit(solution)/shard_map/ppermute | solution.py:179
  56.3 29.2 %copy-start.2 = (bf16[2,1024,512]{2,1,0:T(8,128)(2,1)}, bf16[2,1024,512]{2,1,0:T(8,128)(2,1)S(1)}, u32[]{:S(2)}) copy-start(bf16[2,1024,512]{2,1,0:T(8,128)(2,1)S(1)} %fusion.8.v_ref) | copy-start | bytes 6291460
  84.3 77.1 %collective-permute-start.15 = (bf16[2,256,512]{2,1,0:T(8,128)(2,1)S(1)}, bf16[2,256,512]{2,1,0:T(8,128)(2,1)}, u32[]{:S(2)}, u32[]{:S(2)}) collective-permute-start(bf16[2,256,512]{2,1,0:T(8,128)(2,1)S(1)} %get-tuple-element.155.q_ref.a_ref), channel_id=1, source_target_pairs={{0,2},{1,3},{2,0},{3,1},{4,6},{5,7},{6,4},{7,5},{8,10},{9,11},{10,... | collective-permute-start | bytes 1572872 | tf_op jit(solution)/shard_map/ppermute | solution.py:179
  129.1 28.1 %collective-permute-start.21 = (bf16[2,256,128]{2,1,0:T(8,128)(2,1)S(1)}, bf16[2,256,128]{2,1,0:T(8,128)(2,1)S(1)}, u32[]{:S(2)}, u32[]{:S(2)}) collective-permute-start(bf16[2,256,128]{2,1,0:T(8,128)(2,1)S(1)} %get-tuple-element.159.aq_ref), channel_id=1, source_target_pairs={{0,2},{1,3},{2,0},{3,1},{4,6},{5,7},{6,4},{7,5},{8,10},{9,11},{10,... | collective-permute-start | bytes 393224 | tf_op jit(solution)/shard_map/ppermute | solution.py:179
  129.2 28.4 %collective-permute-start.22 = (bf16[2,256,128]{2,1,0:T(8,128)(2,1)S(1)}, bf16[2,256,128]{2,1,0:T(8,128)(2,1)S(1)}, u32[]{:S(2)}, u32[]{:S(2)}) collective-permute-start(bf16[2,256,128]{2,1,0:T(8,128)(2,1)S(1)} %get-tuple-element.159.aq_ref), channel_id=1, source_target_pairs={{0,1},{1,0},{2,3},{3,2},{4,5},{5,4},{6,7},{7,6},{8,9},{9,8},{10,11... | collective-permute-start | bytes 393224 | tf_op jit(solution)/shard_map/ppermute | solution.py:179
  146.0 36.3 %copy-start.13 = (bf16[2,1024,512]{2,1,0:T(8,128)(2,1)S(1)}, bf16[2,1024,512]{2,1,0:T(8,128)(2,1)}, u32[]{:S(2)}) copy-start(bf16[2,1024,512]{2,1,0:T(8,128)(2,1)} %copy-done.12) | copy-start | bytes 6291460
  150.3 9.1 %collective-permute-start.12 = (bf16[2,256,128]{2,1,0:T(8,128)(2,1)S(1)}, bf16[2,256,128]{2,1,0:T(8,128)(2,1)S(1)}, u32[]{:S(2)}, u32[]{:S(2)}) collective-permute-start(bf16[2,256,128]{2,1,0:T(8,128)(2,1)S(1)} %get-tuple-element.153.aq_ref), channel_id=1, source_target_pairs={{0,2},{1,3},{2,0},{3,1},{4,6},{5,7},{6,4},{7,5},{8,10},{9,11},{10,... | collective-permute-start | bytes 393224 | tf_op jit(solution)/shard_map/ppermute | solution.py:179
  155.0 4.6 collective-permute-start.13
  157.2 25.1 %collective-permute-start.9 = (bf16[2,256,512]{2,1,0:T(8,128)(2,1)S(1)}, bf16[2,256,512]{2,1,0:T(8,128)(2,1)S(1)}, u32[]{:S(2)}, u32[]{:S(2)}) collective-permute-start(bf16[2,256,512]{2,1,0:T(8,128)(2,1)S(1)} %get-tuple-element.151.b_ref), channel_id=1, source_target_pairs={{0,2},{1,3},{2,0},{3,1},{4,6},{5,7},{6,4},{7,5},{8,10},{9,11},{10,... | collective-permute-start | bytes 1572872 | tf_op jit(solution)/shard_map/ppermute | solution.py:179
  157.6 24.7 %collective-permute-start.18 = (bf16[2,256,512]{2,1,0:T(8,128)(2,1)S(1)}, bf16[2,256,512]{2,1,0:T(8,128)(2,1)S(1)}, u32[]{:S(2)}, u32[]{:S(2)}) collective-permute-start(bf16[2,256,512]{2,1,0:T(8,128)(2,1)S(1)} %get-tuple-element.157.b_ref), channel_id=1, source_target_pairs={{0,2},{1,3},{2,0},{3,1},{4,6},{5,7},{6,4},{7,5},{8,10},{9,11},{10,... | collective-permute-start | bytes 1572872 | tf_op jit(solution)/shard_map/ppermute | solution.py:179
  159.4 1.4 collective-permute-start.23
  159.6 1.4 collective-permute-start.14
  160.8 22.2 %collective-permute-start.16 = (bf16[2,256,512]{2,1,0:T(8,128)(2,1)S(1)}, bf16[2,256,512]{2,1,0:T(8,128)(2,1)S(1)}, u32[]{:S(2)}, u32[]{:S(2)}) collective-permute-start(bf16[2,256,512]{2,1,0:T(8,128)(2,1)S(1)} %get-tuple-element.155.q_ref.a_ref), channel_id=1, source_target_pairs={{0,1},{1,0},{2,3},{3,2},{4,5},{5,4},{6,7},{7,6},{8,9},{9,8},{10,11... | collective-permute-start | bytes 1572872 | tf_op jit(solution)/shard_map/ppermute | solution.py:179
  161.0 22.9 %collective-permute-start.10 = (bf16[2,256,512]{2,1,0:T(8,128)(2,1)S(1)}, bf16[2,256,512]{2,1,0:T(8,128)(2,1)S(1)}, u32[]{:S(2)}, u32[]{:S(2)}) collective-permute-start(bf16[2,256,512]{2,1,0:T(8,128)(2,1)S(1)} %get-tuple-element.151.b_ref), channel_id=1, source_target_pairs={{0,1},{1,0},{2,3},{3,2},{4,5},{5,4},{6,7},{7,6},{8,9},{9,8},{10,11... | collective-permute-start | bytes 1572872 | tf_op jit(solution)/shard_map/ppermute | solution.py:179
  161.4 22.5 %collective-permute-start.19 = (bf16[2,256,512]{2,1,0:T(8,128)(2,1)S(1)}, bf16[2,256,512]{2,1,0:T(8,128)(2,1)S(1)}, u32[]{:S(2)}, u32[]{:S(2)}) collective-permute-start(bf16[2,256,512]{2,1,0:T(8,128)(2,1)S(1)} %get-tuple-element.157.b_ref), channel_id=1, source_target_pairs={{0,1},{1,0},{2,3},{3,2},{4,5},{5,4},{6,7},{7,6},{8,9},{9,8},{10,11... | collective-permute-start | bytes 1572872 | tf_op jit(solution)/shard_map/ppermute | solution.py:179
  161.6 25.2 %copy-start.8 = (s32[2,2]{1,0:T(2,128)S(1)}, s32[2,2]{1,0:T(2,128)}, u32[]{:S(2)}) copy-start(s32[2,2]{1,0:T(2,128)} %get-tuple-element.107.count_ref) | copy-start | bytes 52
  182.3 2.1 collective-permute-start.17
  182.3 3.1 collective-permute-start.20
  183.0 12.2 %collective-permute-start.11 = (bf16[2,256,512]{2,1,0:T(8,128)(2,1)S(1)}, bf16[2,256,512]{2,1,0:T(8,128)(2,1)S(1)}, u32[]{:S(2)}, u32[]{:S(2)}) collective-permute-start(bf16[2,256,512]{2,1,0:T(8,128)(2,1)S(1)} %collective-permute-done.9), channel_id=1, source_target_pairs={{0,1},{1,0},{2,3},{3,2},{4,5},{5,4},{6,7},{7,6},{8,9},{9,8},{10,11... | collective-permute-start | bytes 1572872 | tf_op jit(solution)/shard_map/ppermute | solution.py:179
  209.4 56.1 %copy-start.41 = (f32[2,256]{1,0:T(2,128)S(1)}, f32[2,256]{1,0:T(2,128)}, u32[]{:S(2)}) copy-start(f32[2,256]{1,0:T(2,128)} %copy-done.39) | copy-start | bytes 6148
  209.4 56.1 %copy-start.47 = (f32[2,256]{1,0:T(2,128)S(1)}, f32[2,256]{1,0:T(2,128)}, u32[]{:S(2)}) copy-start(f32[2,256]{1,0:T(2,128)} %copy-done.45) | copy-start | bytes 6148
  209.4 56.1 %copy-start.50 = (f32[1,512]{1,0:T(1,128)S(1)}, f32[1,512]{1,0:T(1,128)}, u32[]{:S(2)}) copy-start(f32[1,512]{1,0:T(1,128)} %get-tuple-element.132) | copy-start | bytes 6148
  (84 other events, 518.6 us)
Sparse Core Ops, SparseCore 0:
  209.5 291.8 all-reduce.3

commit v2 on v1

--- a/solution.py
+++ b/solution.py
@@ -244,6 +244,212 @@
     )
 
 
+MESH = pl.DeviceIdType.MESH
+
+
+def dimensions(dp_size, seq_size):
+    dp, seq = lax.axis_index("dp"), lax.axis_index("seq")
+    return {
+        "core": (2, seq % 2, lambda i: (dp, seq - seq % 2 + i)),
+        "y": (seq_size // 2, seq // 2, lambda i: (dp, i * 2 + seq % 2)),
+        "x": (2, dp % 2, lambda i: (dp - dp % 2 + i, seq)),
+        "z": (dp_size // 2, dp // 2, lambda i: (i * 2 + dp % 2, seq)),
+    }
+
+
+ORDERS = (("core", "x", "y", "z"), ("core", "y", "x", "z"))
+
+
+def exchange_sizes(dp_size, seq_size):
+    return {"core": 2, "y": seq_size // 2, "x": 2, "z": dp_size // 2}
+
+
+def sum_kernel(dp_size, seq_size, chunks, src, small, out, small_out, *scratch):
+    dims = dimensions(dp_size, seq_size)
+    stages = 4
+    held = scratch[: chunks * stages]
+    (gathered, small_slots, small_sum, send, recv, small_send, small_recv, save) = scratch[chunks * stages :]
+    total_rows = src.shape[0]
+    rows = total_rows // chunks
+
+    peers = [(name, step) for name in dims for step in range(1, dims[name][0])]
+    barrier = pltpu.get_barrier_semaphore()
+    for name, step in peers:
+        size, me, device = dims[name]
+        pl.semaphore_signal(barrier, inc=1, device_id=device((me + step) % size), device_id_type=MESH)
+    pl.semaphore_wait(barrier, len(peers))
+
+    def reduce_copies(c, s):
+        size, me, device = dims[ORDERS[c % len(ORDERS)][s]]
+        current = src.at[pl.ds(c * rows, rows)] if s == 0 else held[c * stages + s - 1].at[0]
+        piece = current.shape[0] // size
+        copies = []
+        for step in range(1, size):
+            other = (me + step) % size
+            copies.append(
+                pltpu.make_async_remote_copy(
+                    src_ref=current.at[pl.ds(pl.multiple_of(other * piece, piece), piece)],
+                    dst_ref=held[c * stages + s].at[size - step - 1],
+                    send_sem=send.at[c, s, step - 1],
+                    recv_sem=recv.at[c, s, size - step - 1],
+                    device_id=device(other),
+                    device_id_type=MESH,
+                )
+            )
+        return copies
+
+    def offset(c, s):
+        at, extent = c * rows, rows
+        for name in ORDERS[c % len(ORDERS)][:s]:
+            size, me, _ = dims[name]
+            extent //= size
+            at = at + me * extent
+        return pl.multiple_of(at, extent), extent
+
+    def spread_copies(c, s):
+        size, me, device = dims[ORDERS[c % len(ORDERS)][s - 1]]
+        at, extent = offset(c, s)
+        copies = []
+        for step in range(1, size):
+            other = (me + step) % size
+            copies.append(
+                pltpu.make_async_remote_copy(
+                    src_ref=gathered.at[pl.ds(at, extent)],
+                    dst_ref=gathered.at[pl.ds(at, extent)],
+                    send_sem=send.at[c, 2 * stages - s, step - 1],
+                    recv_sem=recv.at[c, 2 * stages - s, size - step - 1],
+                    device_id=device(other),
+                    device_id_type=MESH,
+                )
+            )
+        return copies
+
+    def add_arrived(c, s):
+        size, me, _ = dims[ORDERS[c % len(ORDERS)][s]]
+        current = src.at[pl.ds(c * rows, rows)] if s == 0 else held[c * stages + s - 1].at[0]
+        piece = current.shape[0] // size
+        mine = current.at[pl.ds(pl.multiple_of(me * piece, piece), piece)]
+        block = min(piece, 128)
+        last = s == stages - 1
+        at = offset(c, stages)[0] if last else 0
+
+        def add(i, carry):
+            part = pl.ds(pl.multiple_of(i * block, block), block)
+            value = mine[part].astype(F32)
+            for slot in range(size - 1):
+                value = value + held[c * stages + s][slot, part].astype(F32)
+            if last:
+                gathered[pl.ds(pl.multiple_of(at + i * block, 16), block)] = value.astype(BF)
+            else:
+                held[c * stages + s][0, part] = value.astype(BF)
+            return carry
+
+        lax.fori_loop(0, piece // block, add, 0)
+
+    small_names = ("core", "x", "y", "z")
+
+    def small_copies(s):
+        size, me, device = dims[small_names[s]]
+        copies = []
+        for step in range(1, size):
+            copies.append(
+                pltpu.make_async_remote_copy(
+                    src_ref=small_sum.at[s],
+                    dst_ref=small_slots.at[s, me],
+                    send_sem=small_send.at[s, step - 1],
+                    recv_sem=small_recv.at[s, size - step - 1],
+                    device_id=device((me + step) % size),
+                    device_id_type=MESH,
+                )
+            )
+        return copies
+
+    started = {}
+
+    def begin(key, copies):
+        for copy in copies:
+            copy.start()
+        started[key] = copies
+
+    def finish(key):
+        for copy in started[key]:
+            copy.wait()
+
+    small_sum[0] = small[...]
+    saves = []
+    for wave in range((chunks - 1) // len(ORDERS) + 2 * stages + 1):
+        for c in range(chunks):
+            s = wave - c // len(ORDERS)
+            if s == 0:
+                begin((c, 0), reduce_copies(c, 0))
+            elif 1 <= s <= stages:
+                finish((c, s - 1))
+                add_arrived(c, s - 1)
+                if s < stages:
+                    begin((c, s), reduce_copies(c, s))
+                else:
+                    begin((c, s), spread_copies(c, stages))
+            elif stages < s <= 2 * stages:
+                finish((c, s - 1))
+                if s < 2 * stages:
+                    begin((c, s), spread_copies(c, 2 * stages - s))
+                else:
+                    part = pl.ds(c * rows, rows)
+                    copy = pltpu.make_async_copy(gathered.at[part], out.at[part], save.at[c])
+                    copy.start()
+                    saves.append(copy)
+        if wave <= stages:
+            if wave > 0:
+                finish(("small", wave - 1))
+                size, me, _ = dims[small_names[wave - 1]]
+                small_slots[wave - 1, me] = small_sum[wave - 1]
+                value = small_slots[wave - 1, 0]
+                for i in range(1, size):
+                    value = value + small_slots[wave - 1, i]
+                small_sum[wave] = value
+            if wave < stages:
+                begin(("small", wave), small_copies(wave))
+    small_out[...] = small_sum[stages]
+    for copy in saves:
+        copy.wait()
+
+
+def sum_over_devices(mesh_shape, values, small):
+    dp_size, seq_size = mesh_shape["dp"], mesh_shape["seq"]
+    sizes = exchange_sizes(dp_size, seq_size)
+    total_rows, columns = values.shape
+    per_device = 1
+    for size in sizes.values():
+        per_device *= size
+    chunks = min(16, total_rows // (16 * per_device))
+    most = max(sizes.values())
+    scratch = []
+    for c in range(chunks):
+        extent = total_rows // chunks
+        for name in ORDERS[c % len(ORDERS)]:
+            extent //= sizes[name]
+            scratch.append(pltpu.VMEM((sizes[name] - 1, extent, columns), BF))
+    scratch += [
+        pltpu.VMEM((total_rows, columns), BF),
+        pltpu.VMEM((4, most) + small.shape, F32),
+        pltpu.VMEM((5,) + small.shape, F32),
+        pltpu.SemaphoreType.DMA((chunks, 8, most - 1)),
+        pltpu.SemaphoreType.DMA((chunks, 8, most - 1)),
+        pltpu.SemaphoreType.DMA((4, most - 1)),
+        pltpu.SemaphoreType.DMA((4, most - 1)),
+        pltpu.SemaphoreType.DMA((chunks,)),
+    ]
+    return pl.pallas_call(
+        functools.partial(sum_kernel, dp_size, seq_size, chunks),
+        out_shape=(jax.ShapeDtypeStruct(values.shape, BF), jax.ShapeDtypeStruct(small.shape, F32)),
+        in_specs=[VM, VM],
+        out_specs=(pl.BlockSpec(memory_space=pl.ANY), VM),
+        scratch_shapes=scratch,
+        name="sum_grads",
+        compiler_params=pltpu.CompilerParams(collective_id=0, has_side_effects=True, vmem_limit_bytes=52 << 20),
+    )(values, small)
+
+
 def normalize(residual, gain, shift):
     centred = residual - jnp.mean(residual, axis=-1, keepdims=True)
     inverse_root = lax.rsqrt(jnp.mean(centred * centred, axis=-1, keepdims=True) + EPSILON)
@@ -262,6 +468,7 @@
 
 
 def shards(
+    mesh_shape,
     tokens,
     memory,
     segment_ids,
@@ -414,48 +621,32 @@
     bias_value = token_sum(grad_value)
     grad_self_qkv = weight_grad(tokens, joined)
     grad_tokens = (grad_start + input_grad(joined, self_qkv)).astype(jnp.bfloat16)
-    reduced = lax.psum(
-        (
-            grad_self_qkv,
-            grad_self_out,
-            grad_cross_q,
-            grad_cross_kv,
-            grad_cross_out,
-            grad_ffn_in,
-            grad_ffn_out,
-            jnp.stack([gain_first, gain_second, gain_third]),
-            jnp.stack(
-                [
-                    shift_first,
-                    shift_second,
-                    shift_third,
-                    bias_query,
-                    bias_value,
-                    bias_self_out,
-                    bias_cross_query,
-                    bias_cross_value,
-                    bias_cross_out,
-                    bias_ffn_out,
-                ]
-            ),
-            grad_hbias,
-        ),
-        ("dp", "seq"),
-    )
+    def columns(value):
+        return [value[:, i * 512 : i * 512 + 512] for i in range(value.shape[1] // 512)]
+
+    low = lambda value: value.astype(BF)
+    values = jnp.concatenate(
+        columns(low(grad_self_qkv)) + [low(grad_self_out), low(grad_cross_q)] + columns(low(grad_cross_kv))
+        + [low(grad_cross_out)] + columns(low(grad_ffn_in)) + [low(grad_ffn_out)],
+        axis=0,
+    )
+    small = jnp.concatenate(
+        [
+            jnp.stack([gain_first, gain_second, gain_third, shift_first, shift_second, shift_third, bias_query, bias_value,
+                       bias_self_out, bias_cross_query, bias_cross_value, bias_cross_out, bias_ffn_out]),
+            grad_hbias.reshape(4, 512),
+            jnp.zeros((7, 512), F32),
+        ],
+        axis=0,
+    )
+    values, small = sum_over_devices(mesh_shape, values, small)
+
+    def block(first, count):
+        return jnp.concatenate([values[512 * (first + i) : 512 * (first + i) + 512] for i in range(count)], axis=1).astype(F32)
+
     return (
-        output.astype(jnp.bfloat16),
-        grad_tokens,
-        grad_memory,
-        reduced[0],
-        reduced[1],
-        reduced[2],
-        reduced[3],
-        reduced[4],
-        reduced[5],
-        reduced[6],
-        reduced[7],
-        reduced[8],
-        reduced[9],
+        output.astype(BF), grad_tokens, grad_memory, block(0, 3), block(3, 1), block(4, 1), block(5, 2), block(7, 1), block(8, 4),
+        values[6144:].astype(F32), small[:3], small[3:13], small[13:17].reshape(2048),
     )
 
 
@@ -479,7 +670,7 @@
         P(),
     )
     return jax.shard_map(
-        shards,
+        functools.partial(shards, dict(mesh.shape)),
         mesh=mesh,
         in_specs=placed,
         out_specs=(

time: 534 us -> 330 us (0.62)
  waiting for transfers between devices: 253 us -> 4.16 us
  Pallas kernels: 43.2 us -> 150 us
  blocking collectives: 51.8 us -> 0 us
  other arithmetic: 36.6 us -> 54.7 us
  matrix products: 53 us -> 38 us
  between operations: 15.7 us -> 2.56 us
    psum x1 -> x0, waiting for transfers between devices: 232 us -> none  [shards(): lax.psum((grad_self_qkv, grad_self_out, grad_cross_q, grad_cross_kv, grad...]
    pallas_call x0 -> x1, Pallas kernels: none -> 102 us  [sum_over_devices(): pl.pallas_call(functools.partial(sum_kernel, dp_size, seq_size, chunks),...]
    psum x1 -> x0, blocking collectives: 51.8 us -> none  [shards(): lax.psum((grad_self_qkv, grad_self_out, grad_cross_q, grad_cross_kv, grad...]
    ppermute x24, waiting for transfers between devices: 21.3 us -> 4.16 us  [gather_row(): held[key | bit] = lax.ppermute(held[key], 'seq', swap)]
    dynamic_update_slice x26, local copies, waits for them, and re-layouts: 15.9 us -> 29.4 us  [gather_row(): full = lax.dynamic_update_slice(full, value, at)]
    convert_element_type x0 -> x4, other arithmetic: none -> 10.6 us  [the longest x3 6.21 us: block(): jnp.concatenate([values[512 * (first + i):512 * (first + i) + 512] for i...]
    unnamed x190 -> x220, local copies, waits for them, and re-layouts: 22.3 us -> 12.1 us
    dot_general x7, matrix products: 17.2 us -> 8.6 us  [weight_grad(): jnp.einsum('rtd,rte->de', left, right, preferred_element_type=jnp.float32)]
  transfers between devices with their start and end apart: 25 -> 24, of which waited for: 6 -> 2; matrix products, arithmetic and copies ran while one was open for 19% -> 24% of each run, Pallas kernels for 5% -> 10%
where the time goes in v2:
time: 330 us; the launch traced here: 324 us
  Pallas kernels  150 us (45%)
  local copies, waits for them, and re-layouts  59.2 us (18%)
  other arithmetic  54.7 us (17%)
  matrix products  38 us (12%)
  starting transfers between devices  14.7 us (4%)
  waiting for transfers between devices  4.16 us (1%)
    pallas_call x1, Pallas kernels, sum_over_devices(): pl.pallas_call(functools.partial(sum_kernel, dp_size, seq_size, chunks),...  102 us
    dynamic_update_slice x26, local copies, waits for them, and re-layouts, gather_row(): full = lax.dynamic_update_slice(full, value, at)  29.4 us
    pallas_call x2, Pallas kernels, bwd_dkv(): pl.pallas_call(functools.partial(bwd_kernel, True, tq, width, causal, ahe...  18.8 us
    dot_general x7, matrix products, project(): jnp.einsum('rtd,de->rte', values, weight, preferred_element_type=jnp.floa...  15.4 us
    pallas_call x2, Pallas kernels, bwd_dq(): pl.pallas_call(functools.partial(bwd_kernel, False, tq, width, causal, ah...  15.1 us
    ppermute x24, starting transfers between devices, gather_row(): held[key | bit] = lax.ppermute(held[key], 'seq', swap)  14.7 us
    pallas_call x2, Pallas kernels, fwd(): pl.pallas_call(functools.partial(fwd_kernel, tq, width, causal, ahead), o...  14.2 us
    unnamed x220, local copies, waits for them, and re-layouts  12.1 us
  transfers between devices with their start and end apart: 24, of which 2 were waited for; matrix products, arithmetic and copies ran while one was open for 24% of the time, Pallas kernels for 10%

profile of v2, /device:TPU:0, one launch (start us, length us, event | category | flops | bytes accessed | tf_op | source)
XLA Modules:
  0.0 323.7 jit_solution(15871902925413632097)
XLA Ops:
  1.6 3.0 collective-permute-start
  30.0 2.3 select_convert_fusion
  42.5 1.9 constant_dynamic-update-slice_fusion.24
  44.4 1.9 constant_dynamic-update-slice_fusion.27
  46.2 1.9 constant_dynamic-update-slice_fusion.23
  48.9 5.0 %fusion.29 = f32[2,1024,1536]{2,1,0:T(8,128)S(1)} fusion(bf16[2,1024,512]{2,1,0:T(8,128)(2,1)} %constant_dynamic-update-slice_fusion.26, bf16[512,1536]{1,0:T(8,128)(2,1)S(1)} %copy-done.91), kind=kOutput, calls=%fused_computation.58 | convolution fusion | flops 3221225472 | bytes 16252928 | tf_op jit(solution)/shard_map/rtd,de->rte/dot_general | solution.py:226
  54.3 4.3 %copy-done.27 = f32[2,1024,1536]{2,1,0:T(8,128)} copy-done((f32[2,1024,1536]{2,1,0:T(8,128)}, f32[2,1024,1536]{2,1,0:T(8,128)S(1)}, u32[]{:S(2)}) %copy-start.27) | copy-done | bytes 12582936
  58.5 4.7 %fusion.9 = (bf16[2,1024,512]{2,1,0:T(8,128)(2,1)S(1)}, bf16[2,1024,512]{2,1,0:T(8,128)(2,1)S(1)}) fusion(f32[2,1024,1536]{2,1,0:T(8,128)} %copy-done.27, f32[512]{0:T(512)S(1)} %bitcast.195, f32[512]{0:T(512)S(1)} %bitcast.196), kind=kLoop, calls=%fused_computation.20 | loop fusion | flops 4194304 | bytes 12587008 | tf_op jit(solution)/shard_map/convert_element_type | solution.py:539
  63.3 8.4 %attend_rows.2 = (bf16[2,256,512]{2,1,0:T(8,128)(2,1)S(1)}, bf16[2,256,128]{2,1,0:T(8,128)(2,1)S(1)}) custom-call(s32[2,1]{1,0:T(2,128)S(1)} %get-tuple-element.65.start_ref, s32[2,1]{1,0:T(2,128)S(1)} %get-tuple-element.66.count_ref, s32[1]{0:T(128)} %bitcast.4.base_ref, bf16[2,256,512]{2,1,0:T(8,128)(2,1)S(1)} %constant_dynamic-slice_fusion.4.q_ref.a_ref, ...), custom_call_target="tpu_custom_call" | custom-call | tf_op jit(solution)/shard_map/attend_rows/pallas_call | solution.py:148
  73.5 3.9 %fusion.64 = f32[2,1024,1024]{2,1,0:T(8,128)S(1)} fusion(bf16[2,1024,512]{2,1,0:T(8,128)(2,1)} %constant_dynamic-update-slice_fusion.22, bf16[512,1024]{1,0:T(8,128)(2,1)S(1)} %copy-done.93), kind=kOutput, calls=%fused_computation.97 | convolution fusion | flops 2147483648 | bytes 11534336 | tf_op jit(solution)/shard_map/rtd,de->rte/dot_general | solution.py:226
  81.8 5.9 %attend_rows.3 = (bf16[2,256,512]{2,1,0:T(8,128)(2,1)S(1)}, bf16[2,256,128]{2,1,0:T(8,128)(2,1)S(1)}) custom-call(s32[2,2]{1,0:T(2,128)S(1)} %get-tuple-element.69.start_ref, s32[2,2]{1,0:T(2,128)S(1)} %get-tuple-element.70.count_ref, s32[1]{0:T(128)} %bitcast.4.base_ref, bf16[2,256,512]{2,1,0:T(8,128)(2,1)} %get-tuple-element.122.q_ref.a_ref, ...), custom_call_target="tpu_custom_call" | custom-call | tf_op jit(solution)/shard_map/attend_rows/pallas_call | solution.py:148
  88.7 2.5 fusion.75
  91.2 9.8 %fusion.2 = bf16[2,256,2048]{2,1,0:T(8,128)(2,1)S(1)} fusion(f32[2,256,2048]{2,1,0:T(8,128)S(1)} %get-tuple-element.112, f32[2048]{0:T(1024)S(1)} %copy-done.76, u8[256,2048]{1,0:T(8,128)(4,1)S(1)} %get-tuple-element.34, u8[256,2048]{1,0:T(8,128)(4,1)S(1)} %get-tuple-element.33), kind=kLoop, calls=%fused_computation.5 | loop fusion | flops 74448896 | bytes 7348224 | tf_op jit(solution)/shard_map/convert_element_type | solution.py:564
  105.7 3.2 %convert_reduce_fusion = (f32[2048]{0:T(1024)}, bf16[2,256,2048]{2,1,0:T(8,128)(2,1)S(1)}) fusion(f32[2,256,2048]{2,1,0:T(8,128)S(1)} %get-tuple-element.112, f32[2048]{0:T(1024)S(1)} %copy-done.76, bf16[2,256,512]{2,1,0:T(8,128)(2,1)S(1)} %get-tuple-element.56, bf16[2048,512]{1,0:T(8,128)(2,1)S(1)} %copy-done.90), kind=kOutput, calls=%fused_computation.26 | convolution fusion | flops 1087371264 | bytes 8929280 | tf_op jit(solution)/shard_map/rte,de->rtd/dot_general | solution.py:234
  109.0 2.3 multiply_reduce_fusion
  114.3 2.1 collective-permute-start.22
  119.5 5.2 %query_grad.2 = bf16[2,256,512]{2,1,0:T(8,128)(2,1)S(1)} custom-call(s32[2,2]{1,0:T(2,128)S(1)} %get-tuple-element.69.start_ref, s32[2,2]{1,0:T(2,128)S(1)} %get-tuple-element.70.count_ref, s32[1]{0:T(128)} %bitcast.4.base_ref, bf16[2,256,512]{2,1,0:T(8,128)(2,1)} %get-tuple-element.122.q_ref.a_ref, bf16[2,256,512]{2,1,0:T(8,128)(2,1)S(1)} %get-tuple-element.124.b_ref, ...), custom_call_target="tpu_custom_call" | custom-call | tf_op jit(solution)/shard_map/query_grad/pallas_call | solution.py:153
  130.5 9.9 %query_grad.3 = bf16[2,256,512]{2,1,0:T(8,128)(2,1)S(1)} custom-call(s32[2,1]{1,0:T(2,128)S(1)} %get-tuple-element.65.start_ref, s32[2,1]{1,0:T(2,128)S(1)} %get-tuple-element.66.count_ref, s32[1]{0:T(128)} %bitcast.4.base_ref, bf16[2,256,512]{2,1,0:T(8,128)(2,1)S(1)} %constant_dynamic-slice_fusion.4.q_ref.a_ref, ...), custom_call_target="tpu_custom_call" | custom-call | tf_op jit(solution)/shard_map/query_grad/pallas_call | solution.py:153
  142.3 2.7 bitcast_convert_fusion.1
  155.9 2.0 constant_dynamic-update-slice_fusion.8
  158.2 1.9 constant_dynamic-update-slice_fusion.12
  160.1 2.7 collective-permute-done.9
  168.4 7.8 %key_grad.3 = (bf16[2,256,512]{2,1,0:T(8,128)(2,1)S(1)}, bf16[2,256,512]{2,1,0:T(8,128)(2,1)S(1)}) custom-call(s32[2,2]{1,0:T(2,128)S(1)} %copy-done.14, s32[2,2]{1,0:T(2,128)S(1)} %copy-done.15, s32[1]{0:T(128)} %bitcast.4.base_ref, bf16[2,1024,512]{2,1,0:T(8,128)(2,1)} %constant_dynamic-update-slice_fusion.10.a_ref, ...), custom_call_target="tpu_custom_call" | custom-call | tf_op jit(solution)/shard_map/key_grad/pallas_call | solution.py:158
  177.2 11.0 %key_grad.2 = (bf16[2,256,512]{2,1,0:T(8,128)(2,1)S(1)}, bf16[2,256,512]{2,1,0:T(8,128)(2,1)S(1)}) custom-call(s32[2,1]{1,0:T(2,128)S(1)} %copy-done.16, s32[2,1]{1,0:T(2,128)S(1)} %copy-done.17, s32[1]{0:T(128)} %bitcast.4.base_ref, bf16[2,1024,512]{2,1,0:T(8,128)(2,1)S(1)} %copy-done.5, bf16[2,1024,512]{2,1,0:T(8,128)(2,1)} %constant_dynamic-update-slice_fusion.18.b_ref, ...), custom_call_target="tpu_custom_call" | custom-call | tf_op jit(solution)/shard_map/key_grad/pallas_call | solution.py:158
  191.5 2.0 fusion.36
  196.6 3.3 %copy-done.23 = bf16[8192,512]{1,0:T(8,128)(2,1)} copy-done((bf16[8192,512]{1,0:T(8,128)(2,1)}, bf16[8192,512]{1,0:T(8,128)(2,1)S(1)}, u32[]{:S(2)}) %copy-start.23) | copy-done | bytes 8388632
  200.1 102.2 %sum_grads.1 = (bf16[8192,512]{1,0:T(8,128)(2,1)}, f32[24,512]{1,0:T(8,128)S(1)}) custom-call(bf16[8192,512]{1,0:T(8,128)(2,1)} %copy-done.23, f32[24,512]{1,0:T(8,128)S(1)} %concatenate.24.small), custom_call_target="tpu_custom_call" | custom-call | tf_op jit(solution)/shard_map/sum_grads/pallas_call | solution.py:442
  302.4 4.9 %fusion.145 = (bf16[512,512]{1,0:T(8,128)(2,1)S(1)}, bf16[512,512]{1,0:T(8,128)(2,1)S(1)}, bf16[512,512]{1,0:T(8,128)(2,1)S(1)}, bf16[512,512]{1,0:T(8,128)(2,1)...) fusion(bf16[8192,512]{1,0:T(8,128)(2,1)} %get-tuple-element.31), kind=kLoop, calls=%fused_computation.334 | loop fusion | flops 786432 | bytes 14155776 | tf_op jit(solution)/shard_map/slice | solution.py:645
  307.3 4.4 %slice_convert_fusion.2 = f32[2048,512]{1,0:T(8,128)} fusion(bf16[8192,512]{1,0:T(8,128)(2,1)} %get-tuple-element.31), kind=kLoop, calls=%fused_computation.53 | loop fusion | flops 1048576 | bytes 6291456 | tf_op jit(solution)/shard_map/convert_element_type | solution.py:649
  314.4 2.0 fusion.49
  318.7 2.1 maximum_convert_fusion.1
  320.7 2.6 maximum_convert_fusion
  (382 shorter events, 91.7 us)
Async XLA Ops:
  0.6 88.0 %copy-start = (bf16[512,2048]{1,0:T(8,128)(2,1)S(1)}, bf16[512,2048]{1,0:T(8,128)(2,1)}, u32[]{:S(2)}) copy-start(bf16[512,2048]{1,0:T(8,128)(2,1)} %param.27) | copy-start | bytes 6291460
  0.7 24.0 %copy-start.49 = (s32[2,256]{1,0:T(2,128)S(1)}, s32[2,256]{1,0:T(2,128)}, u32[]{:S(2)}) copy-start(s32[2,256]{1,0:T(2,128)} %param.18) | copy-start | bytes 6148
  1.6 24.7 %collective-permute-start = (s32[2,2,256]{2,1,0:T(2,128)S(1)}, s32[2,2,256]{2,1,0:T(2,128)S(1)}, u32[]{:S(2)}, u32[]{:S(2)}) collective-permute-start(s32[2,2,256]{2,1,0:T(2,128)S(1)} %get-tuple-element.101), channel_id=1, source_target_pairs={{0,2},{1,3},{2,0},{3,1},{4,6},{5,7},{6,4},{7,5},{8,10},{9,11},{10,... | collective-permute-start | bytes 12296 | tf_op jit(solution)/shard_map/ppermute | solution.py:179
  4.5 21.7 %collective-permute-start.1 = (s32[2,2,256]{2,1,0:T(2,128)S(1)}, s32[2,2,256]{2,1,0:T(2,128)S(1)}, u32[]{:S(2)}, u32[]{:S(2)}) collective-permute-start(s32[2,2,256]{2,1,0:T(2,128)S(1)} %get-tuple-element.101), channel_id=1, source_target_pairs={{0,1},{1,0},{2,3},{3,2},{4,5},{5,4},{6,7},{7,6},{8,9},{9,8},{10,11... | collective-permute-start | bytes 12296 | tf_op jit(solution)/shard_map/ppermute | solution.py:179
  4.5 34.2 %collective-permute-start.3 = (bf16[2,256,512]{2,1,0:T(8,128)(2,1)}, bf16[2,256,512]{2,1,0:T(8,128)(2,1)}, u32[]{:S(2)}, u32[]{:S(2)}) collective-permute-start(bf16[2,256,512]{2,1,0:T(8,128)(2,1)} %param.16), channel_id=1, source_target_pairs={{0,2},{1,3},{2,0},{3,1},{4,6},{5,7},{6,4},{7,5},{8,10},{9,11},{10,... | collective-permute-start | bytes 1572872 | tf_op jit(solution)/shard_map/ppermute | solution.py:179
  4.7 39.7 %collective-permute-start.4 = (bf16[2,256,512]{2,1,0:T(8,128)(2,1)}, bf16[2,256,512]{2,1,0:T(8,128)(2,1)}, u32[]{:S(2)}, u32[]{:S(2)}) collective-permute-start(bf16[2,256,512]{2,1,0:T(8,128)(2,1)} %param.16), channel_id=1, source_target_pairs={{0,1},{1,0},{2,3},{3,2},{4,5},{5,4},{6,7},{7,6},{8,9},{9,8},{10,11... | collective-permute-start | bytes 1572872 | tf_op jit(solution)/shard_map/ppermute | solution.py:179
  5.0 35.2 %collective-permute-start.6 = (bf16[2,256,512]{2,1,0:T(8,128)(2,1)}, bf16[2,256,512]{2,1,0:T(8,128)(2,1)}, u32[]{:S(2)}, u32[]{:S(2)}) collective-permute-start(bf16[2,256,512]{2,1,0:T(8,128)(2,1)} %param.17), channel_id=1, source_target_pairs={{0,2},{1,3},{2,0},{3,1},{4,6},{5,7},{6,4},{7,5},{8,10},{9,11},{10,... | collective-permute-start | bytes 1572872 | tf_op jit(solution)/shard_map/ppermute | solution.py:179
  26.2 20.0 %collective-permute-start.7 = (bf16[2,256,512]{2,1,0:T(8,128)(2,1)}, bf16[2,256,512]{2,1,0:T(8,128)(2,1)}, u32[]{:S(2)}, u32[]{:S(2)}) collective-permute-start(bf16[2,256,512]{2,1,0:T(8,128)(2,1)} %param.17), channel_id=1, source_target_pairs={{0,1},{1,0},{2,3},{3,2},{4,5},{5,4},{6,7},{7,6},{8,9},{9,8},{10,11... | collective-permute-start | bytes 1572872 | tf_op jit(solution)/shard_map/ppermute | solution.py:179
  26.3 1.9 collective-permute-start.2
  38.7 9.4 %collective-permute-start.5 = (bf16[2,256,512]{2,1,0:T(8,128)(2,1)}, bf16[2,256,512]{2,1,0:T(8,128)(2,1)S(1)}, u32[]{:S(2)}, u32[]{:S(2)}) collective-permute-start(bf16[2,256,512]{2,1,0:T(8,128)(2,1)} %collective-permute-done.3), channel_id=1, source_target_pairs={{0,1},{1,0},{2,3},{3,2},{4,5},{5,4},{6,7},{7,6},{8,9},{9,8},{10,11... | collective-permute-start | bytes 1572872 | tf_op jit(solution)/shard_map/ppermute | solution.py:179
  40.3 32.3 %collective-permute-start.8 = (bf16[2,256,512]{2,1,0:T(8,128)(2,1)}, bf16[2,256,512]{2,1,0:T(8,128)(2,1)S(1)}, u32[]{:S(2)}, u32[]{:S(2)}) collective-permute-start(bf16[2,256,512]{2,1,0:T(8,128)(2,1)} %collective-permute-done.6), channel_id=1, source_target_pairs={{0,1},{1,0},{2,3},{3,2},{4,5},{5,4},{6,7},{7,6},{8,9},{9,8},{10,11... | collective-permute-start | bytes 1572872 | tf_op jit(solution)/shard_map/ppermute | solution.py:179
  71.7 56.5 %copy-start.12 = (bf16[2,256,512]{2,1,0:T(8,128)(2,1)}, bf16[2,256,512]{2,1,0:T(8,128)(2,1)S(1)}, u32[]{:S(2)}) copy-start(bf16[2,256,512]{2,1,0:T(8,128)(2,1)S(1)} %get-tuple-element.23) | copy-start | bytes 1572868
  72.3 54.0 %copy-start.24 = (f32[2,256,512]{2,1,0:T(8,128)}, f32[2,256,512]{2,1,0:T(8,128)S(1)}, u32[]{:S(2)}) copy-start(f32[2,256,512]{2,1,0:T(8,128)S(1)} %get-tuple-element.109) | copy-start | bytes 3145732
  72.3 54.0 %copy-start.50 = (f32[2,256]{1,0:T(2,128)}, f32[2,256]{1,0:T(2,128)S(1)}, u32[]{:S(2)}) copy-start(f32[2,256]{1,0:T(2,128)S(1)} %broadcast_multiply_fusion.8) | copy-start | bytes 6148
  72.6 53.7 %copy-start.64 = (f32[2,256]{1,0:T(2,128)}, f32[2,256]{1,0:T(2,128)S(1)}, u32[]{:S(2)}) copy-start(f32[2,256]{1,0:T(2,128)S(1)} %add_rsqrt_fusion.2) | copy-start | bytes 6148
  78.8 39.7 %copy-start.2 = (bf16[2,1024,512]{2,1,0:T(8,128)(2,1)}, bf16[2,1024,512]{2,1,0:T(8,128)(2,1)S(1)}, u32[]{:S(2)}) copy-start(bf16[2,1024,512]{2,1,0:T(8,128)(2,1)S(1)} %fusion.8.v_ref) | copy-start | bytes 6291460
  87.7 25.5 %copy-start.18 = (bf16[2,256,512]{2,1,0:T(8,128)(2,1)}, bf16[2,256,512]{2,1,0:T(8,128)(2,1)S(1)}, u32[]{:S(2)}) copy-start(bf16[2,256,512]{2,1,0:T(8,128)(2,1)S(1)} %get-tuple-element.24) | copy-start | bytes 1572868
  114.2 31.6 %collective-permute-start.21 = (bf16[2,256,128]{2,1,0:T(8,128)(2,1)S(1)}, bf16[2,256,128]{2,1,0:T(8,128)(2,1)}, u32[]{:S(2)}, u32[]{:S(2)}) collective-permute-start(bf16[2,256,128]{2,1,0:T(8,128)(2,1)S(1)} %get-tuple-element.126.aq_ref), channel_id=1, source_target_pairs={{0,2},{1,3},{2,0},{3,1},{4,6},{5,7},{6,4},{7,5},{8,10},{9,11},{10,... | collective-permute-start | bytes 393224 | tf_op jit(solution)/shard_map/ppermute | solution.py:179
  114.3 34.7 %collective-permute-start.22 = (bf16[2,256,128]{2,1,0:T(8,128)(2,1)S(1)}, bf16[2,256,128]{2,1,0:T(8,128)(2,1)}, u32[]{:S(2)}, u32[]{:S(2)}) collective-permute-start(bf16[2,256,128]{2,1,0:T(8,128)(2,1)S(1)} %get-tuple-element.126.aq_ref), channel_id=1, source_target_pairs={{0,1},{1,0},{2,3},{3,2},{4,5},{5,4},{6,7},{7,6},{8,9},{9,8},{10,11... | collective-permute-start | bytes 393224 | tf_op jit(solution)/shard_map/ppermute | solution.py:179
  116.4 39.2 %collective-permute-start.18 = (bf16[2,256,512]{2,1,0:T(8,128)(2,1)S(1)}, bf16[2,256,512]{2,1,0:T(8,128)(2,1)}, u32[]{:S(2)}, u32[]{:S(2)}) collective-permute-start(bf16[2,256,512]{2,1,0:T(8,128)(2,1)S(1)} %get-tuple-element.124.b_ref), channel_id=1, source_target_pairs={{0,2},{1,3},{2,0},{3,1},{4,6},{5,7},{6,4},{7,5},{8,10},{9,11},{10,... | collective-permute-start | bytes 1572872 | tf_op jit(solution)/shard_map/ppermute | solution.py:179
  116.8 41.1 %collective-permute-start.15 = (bf16[2,256,512]{2,1,0:T(8,128)(2,1)}, bf16[2,256,512]{2,1,0:T(8,128)(2,1)}, u32[]{:S(2)}, u32[]{:S(2)}) collective-permute-start(bf16[2,256,512]{2,1,0:T(8,128)(2,1)} %get-tuple-element.122.q_ref.a_ref), channel_id=1, source_target_pairs={{0,2},{1,3},{2,0},{3,1},{4,6},{5,7},{6,4},{7,5},{8,10},{9,11},{10,... | collective-permute-start | bytes 1572872 | tf_op jit(solution)/shard_map/ppermute | solution.py:179
  140.4 10.7 %collective-permute-start.12 = (bf16[2,256,128]{2,1,0:T(8,128)(2,1)}, bf16[2,256,128]{2,1,0:T(8,128)(2,1)}, u32[]{:S(2)}, u32[]{:S(2)}) collective-permute-start(bf16[2,256,128]{2,1,0:T(8,128)(2,1)} %get-tuple-element.120.aq_ref), channel_id=1, source_target_pairs={{0,2},{1,3},{2,0},{3,1},{4,6},{5,7},{6,4},{7,5},{8,10},{9,11},{10,... | collective-permute-start | bytes 393224 | tf_op jit(solution)/shard_map/ppermute | solution.py:179
  145.8 7.1 %collective-permute-start.13 = (bf16[2,256,128]{2,1,0:T(8,128)(2,1)}, bf16[2,256,128]{2,1,0:T(8,128)(2,1)S(1)}, u32[]{:S(2)}, u32[]{:S(2)}) collective-permute-start(bf16[2,256,128]{2,1,0:T(8,128)(2,1)} %get-tuple-element.120.aq_ref), channel_id=1, source_target_pairs={{0,1},{1,0},{2,3},{3,2},{4,5},{5,4},{6,7},{7,6},{8,9},{9,8},{10,11... | collective-permute-start | bytes 393224 | tf_op jit(solution)/shard_map/ppermute | solution.py:179
  148.9 13.8 %collective-permute-start.9 = (bf16[2,256,512]{2,1,0:T(8,128)(2,1)S(1)}, bf16[2,256,512]{2,1,0:T(8,128)(2,1)S(1)}, u32[]{:S(2)}, u32[]{:S(2)}) collective-permute-start(bf16[2,256,512]{2,1,0:T(8,128)(2,1)S(1)} %get-tuple-element.118.b_ref), channel_id=1, source_target_pairs={{0,2},{1,3},{2,0},{3,1},{4,6},{5,7},{6,4},{7,5},{8,10},{9,11},{10,... | collective-permute-start | bytes 1572872 | tf_op jit(solution)/shard_map/ppermute | solution.py:179
  151.0 2.8 collective-permute-start.23
  152.8 1.8 collective-permute-start.14
  153.8 9.8 %collective-permute-start.19 = (bf16[2,256,512]{2,1,0:T(8,128)(2,1)S(1)}, bf16[2,256,512]{2,1,0:T(8,128)(2,1)S(1)}, u32[]{:S(2)}, u32[]{:S(2)}) collective-permute-start(bf16[2,256,512]{2,1,0:T(8,128)(2,1)S(1)} %get-tuple-element.124.b_ref), channel_id=1, source_target_pairs={{0,1},{1,0},{2,3},{3,2},{4,5},{5,4},{6,7},{7,6},{8,9},{9,8},{10,11... | collective-permute-start | bytes 1572872 | tf_op jit(solution)/shard_map/ppermute | solution.py:179
  154.7 10.3 %collective-permute-start.16 = (bf16[2,256,512]{2,1,0:T(8,128)(2,1)}, bf16[2,256,512]{2,1,0:T(8,128)(2,1)S(1)}, u32[]{:S(2)}, u32[]{:S(2)}) collective-permute-start(bf16[2,256,512]{2,1,0:T(8,128)(2,1)} %get-tuple-element.122.q_ref.a_ref), channel_id=1, source_target_pairs={{0,1},{1,0},{2,3},{3,2},{4,5},{5,4},{6,7},{7,6},{8,9},{9,8},{10,11... | collective-permute-start | bytes 1572872 | tf_op jit(solution)/shard_map/ppermute | solution.py:179
  155.6 10.2 %collective-permute-start.10 = (bf16[2,256,512]{2,1,0:T(8,128)(2,1)S(1)}, bf16[2,256,512]{2,1,0:T(8,128)(2,1)S(1)}, u32[]{:S(2)}, u32[]{:S(2)}) collective-permute-start(bf16[2,256,512]{2,1,0:T(8,128)(2,1)S(1)} %get-tuple-element.118.b_ref), channel_id=1, source_target_pairs={{0,1},{1,0},{2,3},{3,2},{4,5},{5,4},{6,7},{7,6},{8,9},{9,8},{10,11... | collective-permute-start | bytes 1572872 | tf_op jit(solution)/shard_map/ppermute | solution.py:179
  157.9 8.7 %collective-permute-start.20 = (bf16[2,256,512]{2,1,0:T(8,128)(2,1)}, bf16[2,256,512]{2,1,0:T(8,128)(2,1)S(1)}, u32[]{:S(2)}, u32[]{:S(2)}) collective-permute-start(bf16[2,256,512]{2,1,0:T(8,128)(2,1)} %collective-permute-done.18), channel_id=1, source_target_pairs={{0,1},{1,0},{2,3},{3,2},{4,5},{5,4},{6,7},{7,6},{8,9},{9,8},{10,11... | collective-permute-start | bytes 1572872 | tf_op jit(solution)/shard_map/ppermute | solution.py:179
  162.8 4.7 %collective-permute-start.17 = (bf16[2,256,512]{2,1,0:T(8,128)(2,1)}, bf16[2,256,512]{2,1,0:T(8,128)(2,1)S(1)}, u32[]{:S(2)}, u32[]{:S(2)}) collective-permute-start(bf16[2,256,512]{2,1,0:T(8,128)(2,1)} %collective-permute-done.15), channel_id=1, source_target_pairs={{0,1},{1,0},{2,3},{3,2},{4,5},{5,4},{6,7},{7,6},{8,9},{9,8},{10,11... | collective-permute-start | bytes 1572872 | tf_op jit(solution)/shard_map/ppermute | solution.py:179
  163.6 12.7 %collective-permute-start.11 = (bf16[2,256,512]{2,1,0:T(8,128)(2,1)S(1)}, bf16[2,256,512]{2,1,0:T(8,128)(2,1)S(1)}, u32[]{:S(2)}, u32[]{:S(2)}) collective-permute-start(bf16[2,256,512]{2,1,0:T(8,128)(2,1)S(1)} %collective-permute-done.9), channel_id=1, source_target_pairs={{0,1},{1,0},{2,3},{3,2},{4,5},{5,4},{6,7},{7,6},{8,9},{9,8},{10,11... | collective-permute-start | bytes 1572872 | tf_op jit(solution)/shard_map/ppermute | solution.py:179
  (96 other events, 575.9 us)
